TPU v7x, 256 devices: a whole 4x4x8 slice. The times are simulated.
256 devices in a mesh: dp: 16 (over z, core), expert: 16 (over y, x).
Axes of the slice: x: 4, y: 4, z: 8, core: 2. Of those that a mesh axis runs over, the one named last changes fastest.
Arguments:
- tokens: bfloat16 [2048, 4096], P('expert', 'dp'), may hold values from -6 to 6
- cotangent: bfloat16 [2048, 4096], P('expert', 'dp'), may hold values from -6 to 6
- routing: int32 [2048, 8], P('expert'), may hold values from 0 to 63, all different within a row; in each aligned block of 128 rows (0 to 127, 128 to 255, ...) at most 24 rows name the same one
- w_router: bfloat16 [4096, 64], P('dp'), may hold values from -0.7 to 0.7
- running_mean: bfloat16 [64, 4096], P(None, 'dp'), may hold values from -3 to 3
- w_gate: bfloat16 [64, 4096, 768], P('expert', 'dp'), may hold values from -0.09375 to 0.09375
- w_up: bfloat16 [64, 4096, 768], P('expert', 'dp'), may hold values from -0.09375 to 0.09375
- w_down: bfloat16 [64, 768, 4096], P('expert', None, 'dp'), may hold values from -0.21875 to 0.21875
Outputs:
- grad_tokens: bfloat16 [2048, 4096], P('expert', 'dp')
- grad_router: float32 [4096, 64], P('dp')
- grad_gate: bfloat16 [64, 4096, 768], P('expert', 'dp')
- grad_up: bfloat16 [64, 4096, 768], P('expert', 'dp')
- grad_down: bfloat16 [64, 768, 4096], P('expert', None, 'dp')
Inputs may be any that keep to these rules, and one draw needn't show every extreme that they name: `routing`: each row names 8 different experts. In each aligned block of 128 tokens no expert is named by more than 24 tokens, a bound that some block reaches.
All inputs are finite; a program needn't handle non-finite values.
Results may differ from a plain program's by a relative error of at most 0.035.
Values may be sent and summed in bfloat16 or wider, within the bound.
A program may use at most 192 MiB of HBM per device.

v0:
```python
import jax
import jax.numpy as jnp
from jax import lax
from jax.sharding import PartitionSpec as P


def gate_parts(gate_value):
    sigmoid_gate = jax.nn.sigmoid(gate_value)
    return (gate_value * sigmoid_gate, sigmoid_gate)


def gate_grads(d_hidden, gate_value, up_value, silu_gate, sigmoid_gate):
    d_gate = (
        d_hidden * up_value * sigmoid_gate * (1.0 + gate_value * (1.0 - sigmoid_gate))
    ).astype(jnp.bfloat16)
    d_up = (d_hidden * silu_gate).astype(jnp.bfloat16)
    return (d_gate, d_up)


def per_device(tokens, cotangent, routing, w_router, running_mean, w_gate, w_up, w_down):
    groups = lax.axis_size("expert")
    local_count = w_gate.shape[0]
    experts = groups * local_count
    n_tokens, top_count = routing.shape
    hidden_units = w_gate.shape[2]
    capacity = 3 * n_tokens * top_count // (2 * experts)
    slot_count = experts * capacity
    partial_logits = jnp.dot(tokens, w_router, preferred_element_type=jnp.float32)
    logits = lax.psum(partial_logits, "dp")
    weights_exp = jnp.exp(logits)
    router_prob = weights_exp / jnp.sum(weights_exp, axis=1, keepdims=True)
    flat_route = routing.reshape(-1)
    onehot = (flat_route[:, None] == jnp.arange(experts, dtype=jnp.int32)[None, :]).astype(
        jnp.int32
    )
    before = jnp.cumsum(onehot, axis=0) - onehot
    position = jnp.sum(before * onehot, axis=1)
    slot_id = flat_route * capacity + position
    select = slot_id[:, None] == jnp.arange(slot_count, dtype=jnp.int32)[None, :]
    select_float = select.astype(jnp.float32)
    placing = jnp.sum(
        select.reshape(n_tokens, top_count, slot_count).astype(jnp.int32), axis=1
    ).astype(jnp.bfloat16)
    send_rows = jnp.einsum("ts,td->sd", placing, tokens, preferred_element_type=jnp.float32).astype(
        jnp.bfloat16
    )
    send_grads = jnp.einsum(
        "ts,td->sd", placing, cotangent, preferred_element_type=jnp.float32
    ).astype(jnp.bfloat16)
    onehot_three = onehot.reshape(n_tokens, top_count, experts)
    pair_prob = jnp.sum(router_prob[:, None, :] * onehot_three, axis=2).reshape(-1)
    pair_prob = pair_prob.astype(jnp.bfloat16).astype(jnp.float32)
    send_prob = jnp.dot(pair_prob, select_float, precision=lax.Precision.HIGHEST).astype(
        jnp.bfloat16
    )
    width = tokens.shape[1]
    send_rows = send_rows.reshape(groups, local_count, capacity, width)
    send_grads = send_grads.reshape(groups, local_count, capacity, width)
    send_prob = send_prob.reshape(groups, local_count, capacity)
    got_rows, got_grads, got_prob = (
        lax.all_to_all(send_rows, "expert", split_axis=0, concat_axis=0, tiled=True),
        lax.all_to_all(send_grads, "expert", split_axis=0, concat_axis=0, tiled=True),
        lax.all_to_all(send_prob, "expert", split_axis=0, concat_axis=0, tiled=True),
    )
    gate_part = jnp.einsum("secd,edh->sech", got_rows, w_gate, preferred_element_type=jnp.float32)
    up_part = jnp.einsum("secd,edh->sech", got_rows, w_up, preferred_element_type=jnp.float32)
    joined = jnp.concatenate([gate_part, up_part], axis=3)
    totals = lax.psum(joined.astype(jnp.bfloat16), "dp").astype(jnp.float32)
    gate_value = totals[..., :hidden_units]
    up_value = totals[..., hidden_units:]
    silu_gate, sigmoid_gate = gate_parts(gate_value)
    hidden_act = (silu_gate * up_value).astype(jnp.bfloat16)
    expert_out = jnp.einsum(
        "sech,ehd->secd", hidden_act, w_down, preferred_element_type=jnp.float32
    )
    grads_float = got_grads.astype(jnp.float32)
    slot_dots = jnp.sum(expert_out * grads_float, axis=3).astype(jnp.bfloat16)
    scaled = (got_prob.astype(jnp.float32)[..., None] * grads_float).astype(jnp.bfloat16)
    dh_part = jnp.einsum("secd,ehd->sech", scaled, w_down, preferred_element_type=jnp.float32)
    d_hidden = lax.psum(dh_part.astype(jnp.bfloat16), "dp").astype(jnp.float32)
    d_gate, d_up = gate_grads(d_hidden, gate_value, up_value, silu_gate, sigmoid_gate)
    dx_slots = (
        jnp.einsum("sech,edh->secd", d_gate, w_gate, preferred_element_type=jnp.float32)
        + jnp.einsum("sech,edh->secd", d_up, w_up, preferred_element_type=jnp.float32)
    ).astype(jnp.bfloat16)
    grad_gate = jnp.einsum(
        "secd,sech->edh", got_rows, d_gate, preferred_element_type=jnp.float32
    ).astype(jnp.bfloat16)
    grad_up = jnp.einsum(
        "secd,sech->edh", got_rows, d_up, preferred_element_type=jnp.float32
    ).astype(jnp.bfloat16)
    grad_down = jnp.einsum(
        "sech,secd->ehd", hidden_act, scaled, preferred_element_type=jnp.float32
    ).astype(jnp.bfloat16)
    back_rows, back_dots = (
        lax.all_to_all(dx_slots, "expert", split_axis=0, concat_axis=0, tiled=True),
        lax.all_to_all(slot_dots, "expert", split_axis=0, concat_axis=0, tiled=True),
    )
    back_rows = back_rows.reshape(slot_count, width)
    back_dots = back_dots.reshape(slot_count).astype(jnp.float32)
    dx_experts = jnp.dot(placing, back_rows, preferred_element_type=jnp.float32)
    pair_dots = jnp.dot(select_float, back_dots, precision=lax.Precision.HIGHEST)
    top_dense = jnp.sum(onehot_three * pair_dots.reshape(n_tokens, top_count, 1), axis=1)
    chosen = jnp.sum(onehot_three, axis=1) > 0
    mean_dots = jnp.einsum("td,ed->te", cotangent, running_mean, preferred_element_type=jnp.float32)
    partial_prob = jnp.where(chosen, top_dense, mean_dots)
    d_prob = lax.psum(partial_prob, "dp")
    dlogits = router_prob * (d_prob - jnp.sum(router_prob * d_prob, axis=1, keepdims=True))
    router_part = jnp.einsum(
        "td,te->de", tokens.astype(jnp.float32), dlogits, precision=lax.Precision.HIGHEST
    )
    grad_router = lax.psum(router_part, "expert")
    router_term = jnp.einsum(
        "te,de->td", dlogits, w_router.astype(jnp.float32), precision=lax.Precision.HIGHEST
    )
    grad_tokens = (dx_experts + router_term).astype(jnp.bfloat16)
    return (grad_tokens, grad_router, grad_gate, grad_up, grad_down)


def solution(mesh):
    placed = (
        P("expert", "dp"),
        P("expert", "dp"),
        P("expert", None),
        P("dp", None),
        P(None, "dp"),
        P("expert", "dp", None),
        P("expert", "dp", None),
        P("expert", None, "dp"),
    )
    return jax.shard_map(
        per_device,
        mesh=mesh,
        in_specs=placed,
        out_specs=(
            P("expert", "dp"),
            P("dp", None),
            P("expert", "dp", None),
            P("expert", "dp", None),
            P("expert", None, "dp"),
        ),
        check_vma=False,
    )
```

profile of v0, /device:TPU:2, one launch (start us, length us, event | category | flops | bytes accessed | tf_op | source)
XLA Modules:
  0.0 448.4 jit_solution(11008265748631963824)
XLA Ops:
  7.2 0.9 copy.109
  8.4 18.0 %reduce-window.6 = s32[64,8,128]{2,1,0:T(8,128)S(1)} reduce-window(s32[64,8,128]{2,1,0:T(8,128)S(1)} %fusion.50, s32[]{:T(128)} %constant.5.clone.1), window={size=1x1x128 pad=0_0x0_0x127_0}, to_apply=%region_0.0 | reduce-window | flops 8323072 | bytes 524292 | tf_op jit(solution)/shard_map/reduce-window
  27.3 2.5 convert_reduce_fusion
  30.2 20.2 %all_to_all.25 = bf16[16,4,24,256]{3,2,1,0:T(8,128)(2,1)S(1)} all-to-all(bf16[16,4,24,256]{3,2,1,0:T(8,128)(2,1)S(1)} %bitcast.89), channel_id=1, replica_groups=mesh['dp'=16,'expert'=16] {'expert'}, dimensions={0} | all-to-all | bytes 1572864 | tf_op jit(solution)/shard_map/all_to_all | solution.py:61
  52.1 2.6 pad_maximum_fusion
  55.6 2.4 convolution_convert_fusion.1
  58.0 5.5 %all-to-all-start.1 = ((bf16[16,4,24,256]{3,2,1,0:T(8,128)(2,1)}), bf16[16,4,24,256]{3,2,1,0:T(8,128)(2,1)}, u32[]{:S(2)}, u32[]{:S(2)}) async-start(bf16[16,4,24,256]{3,2,1,0:T(8,128)(2,1)} %bitcast.88), calls=%async_computation.1 | async-start | bytes 1572864 | tf_op jit(solution)/shard_map/all_to_all | solution.py:62
  63.6 49.9 %psum.35 = f32[128,64]{0,1:T(8,128)S(1)} all-reduce(f32[128,64]{0,1:T(8,128)S(1)} %fusion.55), channel_id=1, replica_groups=mesh['dp'=16,'expert'=16] {'dp'}, use_global_device_ids=true, to_apply=%region_4.5 | all-reduce | flops 8192 | bytes 65536 | tf_op jit(solution)/shard_map/psum | solution.py:29
  113.5 65.1 %all-reduce.6.cloned.1.call-done = bf16[16,4,24,1536]{3,2,0,1:T(8,128)(2,1)} async-done(((bf16[16,4,24,1536]{3,2,0,1:T(8,128)(2,1)}), bf16[16,4,24,1536]{3,2,0,1:T(8,128)(2,1)}) %all-reduce.6.cloned.1.call-update) | async-done | bytes 4718608 | tf_op jit(solution)/shard_map/psum | solution.py:68
  178.6 3.6 convert_element_type.109
  182.3 3.6 copy-done.1
  185.9 2.6 multiply_convert_fusion
  188.5 3.3 fusion.20
  192.3 7.3 %all-to-all-start.4 = ((bf16[16,4,24]{2,1,0:T(4,128)(2,1)}), bf16[16,4,24]{2,1,0:T(4,128)(2,1)S(1)}, u32[]{:S(2)}, u32[]{:S(2)}) async-start(bf16[16,4,24]{2,1,0:T(4,128)(2,1)} %copy.122), calls=%async_computation.4 | async-start | bytes 32768 | tf_op jit(solution)/shard_map/all_to_all | solution.py:97
  199.9 6.0 %all-to-all-done.4 = bf16[16,4,24]{2,1,0:T(4,128)(2,1)S(1)} async-done(((bf16[16,4,24]{2,1,0:T(4,128)(2,1)}), bf16[16,4,24]{2,1,0:T(4,128)(2,1)S(1)}, u32[]{:S(2)}, u32[]{:S(2)}) %all-to-all-start.4) | async-done | bytes 3104 | tf_op jit(solution)/shard_map/all_to_all | solution.py:97
  205.9 7.1 %fusion.2 = f32[1,128,8]{2,0,1:T(1,128)S(1)} fusion(bf16[1536,1,1]{0,1,2:T(2,128)(2,1)S(1)} %reshape.117, s32[128,8]{1,0:T(8,128)S(1)} %copy.114), kind=kOutput, calls=%fused_computation.6 | convolution fusion | flops 4718592 | bytes 11264 | tf_op jit(solution)/shard_map/dot_general | solution.py:102
  213.4 1.3 fusion.36
  214.8 10.6 %all_to_all.26 = bf16[16,4,24]{2,1,0:T(4,128)(2,1)S(1)} all-to-all(bf16[16,4,24]{2,1,0:T(4,128)(2,1)S(1)} %reshape.107), channel_id=1, replica_groups=mesh['dp'=16,'expert'=16] {'expert'}, dimensions={0} | all-to-all | bytes 6144 | tf_op jit(solution)/shard_map/all_to_all | solution.py:63
  225.4 3.9 convert_bitcast_fusion.2
  230.2 45.7 %psum.38 = f32[128,64]{0,1:T(8,128)S(1)} all-reduce(f32[128,64]{0,1:T(8,128)S(1)} %convolution_select_fusion), channel_id=1, replica_groups=mesh['dp'=16,'expert'=16] {'dp'}, use_global_device_ids=true, to_apply=%region_12.13 | all-reduce | flops 8192 | bytes 65536 | tf_op jit(solution)/shard_map/psum | solution.py:107
  277.1 4.4 bitcast_convert_fusion
  281.4 61.2 %all-reduce.4.cloned.1.call-done = bf16[16,4,24,768]{3,2,0,1:T(8,128)(2,1)} async-done(((bf16[16,4,24,768]{3,2,0,1:T(8,128)(2,1)}), bf16[16,4,24,768]{3,2,0,1:T(8,128)(2,1)}) %all-reduce.4.cloned.1.call-update) | async-done | bytes 2359312 | tf_op jit(solution)/shard_map/psum | solution.py:80
  342.7 5.7 %fusion.7 = (bf16[16,4,24,768]{3,2,0,1:T(8,128)(2,1)S(1)}, bf16[16,4,24,768]{3,2,0,1:T(8,128)(2,1)S(1)}) fusion(bf16[16,4,24,768]{3,2,0,1:T(8,128)(2,1)} %all-reduce.4.cloned.1.call-done, f32[16,4,24,1536]{3,2,0,1:T(8,128)} %copy-done.1), kind=kLoop, calls=%fused_computation.12 | loop fusion | flops 16515072 | bytes 16515072 | tf_op jit(solution)/shard_map/convert_element_type | solution.py:16
  350.5 0.8 fusion.32
  351.3 1.0 copy.120
  352.4 7.3 %all-to-all-start.3 = ((bf16[16,4,24,256]{3,2,1,0:T(8,128)(2,1)}), bf16[16,4,24,256]{3,2,1,0:T(8,128)(2,1)}, u32[]{:S(2)}, u32[]{:S(2)}) async-start(bf16[16,4,24,256]{3,2,1,0:T(8,128)(2,1)} %copy.120), calls=%async_computation.3 | async-start | bytes 1572864 | tf_op jit(solution)/shard_map/all_to_all | solution.py:96
  359.7 4.0 bitcast_convert_fusion.1
  363.7 2.2 bitcast_convert_fusion.2
  365.9 6.6 %all-to-all-done.3 = bf16[16,4,24,256]{3,2,1,0:T(8,128)(2,1)} async-done(((bf16[16,4,24,256]{3,2,1,0:T(8,128)(2,1)}), bf16[16,4,24,256]{3,2,1,0:T(8,128)(2,1)}, u32[]{:S(2)}, u32[]{:S(2)}) %all-to-all-start.3) | async-done | bytes 786464 | tf_op jit(solution)/shard_map/all_to_all | solution.py:96
  372.5 2.0 fusion.35
  374.5 65.8 %all-reduce.8.cloned.1.call-done = f32[256,64]{0,1:T(8,128)} async-done(((f32[256,64]{0,1:T(8,128)}), f32[256,64]{0,1:T(8,128)}) %all-reduce.8.cloned.1.call-update) | async-done | bytes 65552 | tf_op jit(solution)/shard_map/psum | solution.py:112
  440.4 1.5 copy.152
  (71 shorter events, 9.7 us)
Async XLA Ops:
  7.2 44.2 %copy-start = (bf16[4,256,768]{2,1,0:T(8,128)(2,1)S(1)}, bf16[4,256,768]{2,1,0:T(8,128)(2,1)}, u32[]{:S(2)}) copy-start(bf16[4,256,768]{2,1,0:T(8,128)(2,1)} %param.13) | copy-start | bytes 4718596
  7.2 20.0 %copy-start.13 = (s32[128,8]{0,1:T(8,128)S(1)}, s32[128,8]{0,1:T(8,128)}, u32[]{:S(2)}) copy-start(s32[128,8]{0,1:T(8,128)} %param.10) | copy-start | bytes 12292
  7.2 22.6 %copy-start.10 = (bf16[128,256]{1,0:T(8,128)(2,1)S(1)}, bf16[128,256]{1,0:T(8,128)(2,1)}, u32[]{:S(2)}) copy-start(bf16[128,256]{1,0:T(8,128)(2,1)} %param.8) | copy-start | bytes 196612
  7.2 171.4 %all-reduce.6.cloned.1.call-start = ((), (), s32[]{:S(2)}) async-start(), calls=%async_computation.6 | async-start | bytes 9437184 | tf_op jit(solution)/shard_map/psum | solution.py:68
  26.9 23.6 %copy-start.5 = (bf16[4,256,768]{2,1,0:T(8,128)(2,1)S(1)}, bf16[4,256,768]{2,1,0:T(8,128)(2,1)}, u32[]{:S(2)}) copy-start(bf16[4,256,768]{2,1,0:T(8,128)(2,1)} %param.14) | copy-start | bytes 4718596
  29.8 21.5 %copy-start.8 = (s32[128,1536]{1,0:T(8,128)}, s32[128,1536]{1,0:T(8,128)S(1)}, u32[]{:S(2)}) copy-start(s32[128,1536]{1,0:T(8,128)S(1)} %convert_reduce_fusion) | copy-start | bytes 2359300
  50.5 0.9 copy-start.6
  54.7 0.8 copy-start.11
  55.6 7.9 %copy-start.12 = (bf16[256,64]{0,1:T(8,128)(2,1)S(1)}, bf16[256,64]{0,1:T(8,128)(2,1)}, u32[]{:S(2)}) copy-start(bf16[256,64]{0,1:T(8,128)(2,1)} %param.11) | copy-start | bytes 98308
  58.0 130.5 %all-to-all-start.1 = ((bf16[16,4,24,256]{3,2,1,0:T(8,128)(2,1)}), bf16[16,4,24,256]{3,2,1,0:T(8,128)(2,1)}, u32[]{:S(2)}, u32[]{:S(2)}) async-start(bf16[16,4,24,256]{3,2,1,0:T(8,128)(2,1)} %bitcast.88), calls=%async_computation.1 | async-start | bytes 1572864 | tf_op jit(solution)/shard_map/all_to_all | solution.py:62
  182.3 3.6 copy-start.1
  192.3 13.5 %all-to-all-start.4 = ((bf16[16,4,24]{2,1,0:T(4,128)(2,1)}), bf16[16,4,24]{2,1,0:T(4,128)(2,1)S(1)}, u32[]{:S(2)}, u32[]{:S(2)}) async-start(bf16[16,4,24]{2,1,0:T(4,128)(2,1)} %copy.122), calls=%async_computation.4 | async-start | bytes 32768 | tf_op jit(solution)/shard_map/all_to_all | solution.py:97
  199.6 143.1 %all-reduce.4.cloned.1.call-start = ((), (), s32[]{:S(2)}) async-start(), calls=%async_computation.5 | async-start | bytes 4718592 | tf_op jit(solution)/shard_map/psum | solution.py:80
  229.3 0.8 copy-start.14
  229.3 211.0 %all-reduce.8.cloned.1.call-start = ((), (), s32[]{:S(2)}) async-start(), calls=%async_computation.7 | async-start | bytes 131072 | tf_op jit(solution)/shard_map/psum | solution.py:112
  348.4 1.4 copy-start.3
  348.4 2.1 copy-start.2
  351.3 8.3 %copy-start.7 = (bf16[16,4,24,256]{3,2,1,0:T(8,128)(2,1)S(1)}, bf16[16,4,24,256]{3,2,1,0:T(8,128)(2,1)}, u32[]{:S(2)}) copy-start(bf16[16,4,24,256]{3,2,1,0:T(8,128)(2,1)} %copy-done.6) | copy-start | bytes 2359300
  352.4 20.1 %all-to-all-start.3 = ((bf16[16,4,24,256]{3,2,1,0:T(8,128)(2,1)}), bf16[16,4,24,256]{3,2,1,0:T(8,128)(2,1)}, u32[]{:S(2)}, u32[]{:S(2)}) async-start(bf16[16,4,24,256]{3,2,1,0:T(8,128)(2,1)} %copy.120), calls=%async_computation.3 | async-start | bytes 1572864 | tf_op jit(solution)/shard_map/all_to_all | solution.py:96
  359.7 4.0 copy-start.4
  363.7 8.8 %copy-start.9 = (s32[128,1536]{1,0:T(8,128)S(1)}, s32[128,1536]{1,0:T(8,128)}, u32[]{:S(2)}) copy-start(s32[128,1536]{1,0:T(8,128)} %copy-done.8) | copy-start | bytes 2359300
Sparse Core Ops, SparseCore 0:
  54.9 123.6 all-reduce.5
  229.4 113.1 all-reduce.3
  346.4 93.8 all-reduce.7
where the time goes:
time: 449 us; the launch traced here: 448 us
  waiting for transfers between devices  205 us (46%)
  blocking collectives  126 us (28%)
  other arithmetic  35.5 us (8%)
  matrix products  35.5 us (8%)
  starting transfers between devices  20.3 us (5%)
  between operations  14 us (3%)
  local copies, waits for them, and re-layouts  11.8 us (3%)
    psum x1, waiting for transfers between devices, per_device(): grad_router = lax.psum(router_part, 'expert')  65.8 us
    psum x1, waiting for transfers between devices, per_device(): totals = lax.psum(joined.astype(jnp.bfloat16), 'dp').astype(jnp.float32)  65.1 us
    psum x1, waiting for transfers between devices, per_device(): d_hidden = lax.psum(dh_part.astype(jnp.bfloat16), 'dp').astype(jnp.float32)  61.2 us
    psum x1, blocking collectives, per_device(): logits = lax.psum(partial_logits, 'dp')  49.9 us
    psum x1, blocking collectives, per_device(): d_prob = lax.psum(partial_prob, 'dp')  45.7 us
    all_to_all x1, blocking collectives, per_device(): lax.all_to_all(send_rows, 'expert', split_axis=0, concat_axis=0, tiled=True)  20.2 us
    another operation x3, other arithmetic  18.2 us
    all_to_all x1, blocking collectives, per_device(): lax.all_to_all(send_prob, 'expert', split_axis=0, concat_axis=0, tiled=True)  10.6 us
  transfers between devices with their start and end apart: 6, of which 5 were waited for; matrix products, arithmetic and copies ran while one was open for 7% of the time, Pallas kernels for 0%

commit v1 on v0

v1 whole, which is shorter than its diff:
```python
import functools

import jax
import jax.numpy as jnp
from jax import lax
from jax.experimental import pallas as pl
from jax.experimental.pallas import tpu as pltpu
from jax.sharding import PartitionSpec as P

MESH = pl.DeviceIdType.MESH
BF = jnp.bfloat16
F32 = jnp.float32
CORES = 2
RS_LAG = 2
AG_LAG = 3


def rem(a, n):
    return lax.rem(a, jnp.int32(n))


def div(a, n):
    return lax.div(a, jnp.int32(n))


def remote(src, dst, send_sem, recv_sem, device):
    return pltpu.make_async_remote_copy(
        src_ref=src,
        dst_ref=dst,
        send_sem=send_sem,
        recv_sem=recv_sem,
        device_id=device,
        device_id_type=MESH,
    )


def loop(lower, upper, body):
    def step(i, carry):
        body(i)
        return carry

    lax.fori_loop(lower, upper, step, 0)


def dot_nn(a, b):
    return jnp.dot(a, b, preferred_element_type=F32)


def dot_nt(a, b):
    return lax.dot_general(a, b, (((1,), (1,)), ((), ())), preferred_element_type=F32)


def dot_tn(a, b):
    return lax.dot_general(a, b, (((0,), (0,)), ((), ())), preferred_element_type=F32)


def split_two(value):
    high = value.astype(BF)
    low = (value - high.astype(F32)).astype(BF)
    return high, low


def kernel(
    sizes,
    tokens, cotangent, routing, w_router, running_mean, w_gate, w_up, w_down,
    grad_tokens, grad_router, grad_gate, grad_up, grad_down,
    place, send_rows, in_rows, rows, wg, wu, wd,
    part, recv, full,
    sum_src, sum_in, sum_out, gr_src, gr_in, gr_out,
    prob_ref, w_send, w_in, dots_send, dots_in, top_send, top_in, dlog_hi, dlog_lo,
    dx_ref, back_send, back_in, out_gate, out_up, out_down,
    rows_s, rows_r, wx_s, wx_r, wl_s,
    p1_s, p1_r, p2_s, p2_r,
    rs_s, rs_r, ag_s, ag_r,
    wt_s, wt_r, dt_s, dt_r, tp_s, tp_r, bk_s, bk_r,
    ol_s, ox_s, ox_r,
):
    NE, Z, E, TOK, H, W, CAP = sizes
    ND = Z * CORES
    NQ = NE * CORES
    S = NE // Z
    HH = H // 2
    EL = 64
    PAIR = 2 * CAP
    ROWS = NE * CAP

    dp = lax.axis_index("dp")
    xy = lax.axis_index("expert")
    z = div(dp, CORES)
    c = rem(dp, CORES)
    other = 1 - c
    q = xy * CORES + c
    right = rem(z + 1, Z)
    left = rem(z + Z - 1, Z)
    twin = (z * CORES + other, xy)

    def plane_peer(q2):
        return (z * CORES + rem(q2, CORES), div(q2, CORES))

    barrier = pltpu.get_barrier_semaphore()

    def greet_plane(k):
        pl.semaphore_signal(
            barrier, inc=1, device_id=plane_peer(rem(q + k, NQ)), device_id_type=MESH
        )

    def greet_column(m):
        z2 = rem(z + 1 + div(m, CORES), Z)
        pl.semaphore_signal(
            barrier, inc=1, device_id=(z2 * CORES + rem(m, CORES), xy), device_id_type=MESH
        )

    loop(1, NQ, greet_plane)
    loop(0, CORES * (Z - 1), greet_column)

    def own_weights(i, src, dst):
        return pltpu.make_async_copy(src, dst, wl_s.at[i])

    half = pl.ds(pl.multiple_of(c * W, W), W)
    mine = pl.ds(c * 2, 2)
    theirs = pl.ds(other * 2, 2)
    own_copies = [
        own_weights(0, w_gate.at[mine], wg.at[:, half, :]),
        own_weights(1, w_up.at[mine], wu.at[:, half, :]),
        own_weights(2, w_down.at[mine], wd.at[c]),
    ]
    for copy in own_copies:
        copy.start()

    route = routing[...]
    lane = lax.broadcasted_iota(jnp.int32, (TOK, E), 1)
    chosen = jnp.zeros((TOK, E), F32)
    for k in range(route.shape[1]):
        chosen = chosen + jnp.where(route[:, k : k + 1] == lane, 1.0, 0.0)
    chosen_b = chosen.astype(BF)
    t_row = lax.broadcasted_iota(jnp.int32, (TOK, TOK), 0)
    t_col = lax.broadcasted_iota(jnp.int32, (TOK, TOK), 1)
    before = jnp.where(t_row < t_col, 1.0, 0.0).astype(BF)
    same = jnp.where(t_row == t_col, 1.0, 0.0).astype(BF)
    pos = dot_tn(chosen_b, before)
    has = dot_tn(chosen_b, same)
    pos = jnp.where(has > 0.5, pos, -1.0)
    slot_iota = lax.broadcasted_iota(jnp.int32, (E, CAP, TOK), 1).astype(F32)
    placing = jnp.where(pos[:, None, :] == slot_iota, 1.0, 0.0)
    placing = placing.reshape(E * CAP, TOK).astype(BF)
    place[...] = placing.reshape(NE, CORES, PAIR, TOK)
    send_rows[0] = dot_nn(placing, tokens[...]).astype(BF).reshape(NQ, PAIR, W)
    send_rows[1] = dot_nn(placing, cotangent[...]).astype(BF).reshape(NQ, PAIR, W)

    pl.semaphore_wait(barrier, NQ - 1 + CORES * (Z - 1))

    def rows_copy(which, q2):
        return remote(
            send_rows.at[which, q2], in_rows.at[which, c, xy],
            rows_s.at[which, q2], rows_r.at[which, q], plane_peer(q2),
        )

    def rows_arrival(which, q2):
        return remote(
            send_rows.at[which, q2], in_rows.at[which, rem(q2, CORES), div(q2, CORES)],
            rows_s.at[which, q2], rows_r.at[which, q2], plane_peer(q2),
        )

    weight_copies = [
        remote(w_gate.at[theirs], wg.at[:, half, :], wx_s.at[0], wx_r.at[0], twin),
        remote(w_up.at[theirs], wu.at[:, half, :], wx_s.at[1], wx_r.at[1], twin),
        remote(w_down.at[theirs], wd.at[c], wx_s.at[2], wx_r.at[2], twin),
    ]
    other_half = pl.ds(pl.multiple_of(other * W, W), W)
    weight_arrivals = [
        remote(w_gate.at[theirs], wg.at[:, other_half, :], wx_s.at[0], wx_r.at[0], twin),
        remote(w_up.at[theirs], wu.at[:, other_half, :], wx_s.at[1], wx_r.at[1], twin),
        remote(w_down.at[theirs], wd.at[other], wx_s.at[2], wx_r.at[2], twin),
    ]
    weight_copies[0].start()
    weight_copies[1].start()
    loop(1, NQ, lambda k: rows_copy(0, rem(q + k, NQ)).start())
    loop(1, NQ, lambda k: rows_copy(1, rem(q + k, NQ)).start())
    weight_copies[2].start()
    in_rows[0, c, xy] = send_rows[0, q]
    in_rows[1, c, xy] = send_rows[1, q]

    def sum_blocks(n, index, peer, src, into, out, sem_s, sem_r):
        def scatter(j):
            return remote(src.at[j], into.at[index], sem_s.at[0, j], sem_r.at[0, index], peer(j))

        def scatter_arrival(j):
            return remote(src.at[j], into.at[j], sem_s.at[0, j], sem_r.at[0, j], peer(j))

        def gather(j):
            return remote(
                out.at[index], out.at[index], sem_s.at[1, j], sem_r.at[1, index], peer(j)
            )

        def gather_arrival(j):
            return remote(out.at[j], out.at[j], sem_s.at[1, j], sem_r.at[1, j], peer(j))

        def send():
            loop(1, n, lambda k: scatter(rem(index + k, n)).start())
            into[index] = src[index]

        def reduce():
            loop(1, n, lambda k: scatter_arrival(rem(index + k, n)).wait_recv())
            out[index] = jnp.sum(into[...], axis=0)
            loop(1, n, lambda k: gather(rem(index + k, n)).start())

        def finish():
            loop(1, n, lambda k: gather_arrival(rem(index + k, n)).wait_recv())

        def drain():
            loop(1, n, lambda k: scatter(rem(index + k, n)).wait_send())
            loop(1, n, lambda k: gather(rem(index + k, n)).wait_send())

        return send, reduce, finish, drain

    p1_send, p1_reduce, p1_finish, p1_drain = sum_blocks(
        ND, dp, lambda j: (j, xy), sum_src, sum_in, sum_out, p1_s, p1_r
    )
    p2_send, p2_reduce, p2_finish, p2_drain = sum_blocks(
        NE, xy, lambda j: (dp, j), gr_src, gr_in, gr_out, p2_s, p2_r
    )

    def packed(first, second, count):
        if E < EL:
            gap = jnp.zeros((TOK, EL - E), F32)
            first = jnp.concatenate([first, gap], axis=1)
            second = jnp.concatenate([second, gap], axis=1)
        return jnp.concatenate([first, second], axis=1).reshape(count, TOK // count, 2 * EL)

    logits_part = dot_nn(tokens[...], w_router[...])
    mean_part = dot_nt(cotangent[...], running_mean[...])
    sum_src[...] = packed(logits_part, mean_part, ND)
    p1_send()

    def order_rows(which):
        def body(p):
            for h in range(CORES):
                block = in_rows[which, h, pl.ds(p * 2, 2)].astype(F32)
                for j in range(2):
                    piece = block[:, j * CAP : (j + 1) * CAP, :].reshape(PAIR, W)
                    rows[
                        which, j, pl.ds(pl.multiple_of(p * PAIR, PAIR), PAIR), h * W : (h + 1) * W
                    ] = piece.astype(BF)

        loop(0, NE // 2, body)

    def rs_copy(k, r, s):
        t = rem(z - 1 - s + 2 * Z, Z) if r == 0 else rem(z + 1 + s, Z)
        peer = ((right if r == 0 else left) * CORES + c, xy)
        return remote(
            part.at[k, r, t], recv.at[k, r, s], rs_s.at[k, r, s], rs_r.at[k, r, s], peer
        )

    def rs_step(k, r, s):
        rs_copy(k, r, s).wait_recv()
        t = rem(z - 2 - s + 2 * Z, Z) if r == 0 else rem(z + 2 + s, Z)
        part[k, r, t] = (part[k, r, t].astype(F32) + recv[k, r, s].astype(F32)).astype(BF)
        rs_copy(k, r, s + 1).start()

    def ag_copy(k, r, s):
        t = rem(z - s + Z, Z) if r == 0 else rem(z + s, Z)
        peer = ((right if r == 0 else left) * CORES + c, xy)
        return remote(
            full.at[k, r, t], full.at[k, r, t], ag_s.at[k, r, s], ag_r.at[k, r, s], peer
        )

    def ag_arrival(k, r, s):
        t = rem(z - 1 - s + Z, Z) if r == 0 else rem(z + 1 + s, Z)
        peer = ((right if r == 0 else left) * CORES + c, xy)
        return remote(
            full.at[k, r, t], full.at[k, r, t], ag_s.at[k, r, s], ag_r.at[k, r, s], peer
        )

    def ag_step(k, r, s):
        ag_arrival(k, r, s).wait_recv()
        ag_copy(k, r, s + 1).start()

    own_copies[0].wait()
    own_copies[1].wait()
    weight_arrivals[0].wait_recv()
    weight_arrivals[1].wait_recv()
    loop(1, NQ, lambda k: rows_arrival(0, rem(q + k, NQ)).wait_recv())
    order_rows(0)
    for j in range(2):
        for r in range(2):
            cols = slice(r * HH, (r + 1) * HH)
            part[j, r, :, :, 0:HH] = (
                dot_nn(rows[0, j], wg[j, :, cols]).astype(BF).reshape(Z, S * CAP, HH)
            )
            part[j, r, :, :, HH:H] = (
                dot_nn(rows[0, j], wu[j, :, cols]).astype(BF).reshape(Z, S * CAP, HH)
            )
            rs_copy(j, r, 0).start()

    p1_reduce()

    own_copies[2].wait()
    weight_arrivals[2].wait_recv()
    loop(1, NQ, lambda k: rows_arrival(1, rem(q + k, NQ)).wait_recv())
    order_rows(1)
    for r in range(2):
        units = slice(r * HH, (r + 1) * HH)
        for j in range(2):
            value = dot_nt(rows[1, j, :, 0:W], wd[0, j, units, :]) + dot_nt(
                rows[1, j, :, W : 2 * W], wd[1, j, units, :]
            )
            part[2, r, :, :, j * HH : (j + 1) * HH] = value.astype(BF).reshape(Z, S * CAP, HH)
        rs_copy(2, r, 0).start()

    p1_finish()
    sums = sum_out[...].reshape(TOK, 2 * EL)
    weights_exp = jnp.exp(sums[:, 0:E])
    prob_ref[...] = weights_exp / jnp.sum(weights_exp, axis=1, keepdims=True)

    slot_row = lax.broadcasted_iota(jnp.int32, (NE, PAIR, 2 * EL), 1)
    slot_owner = lax.broadcasted_iota(jnp.int32, (NE, PAIR, 2 * EL), 0)
    slot_lane = lax.broadcasted_iota(jnp.int32, (NE, PAIR, 2 * EL), 2)
    slot_expert = slot_owner * 4 + c * 2 + jnp.where(slot_row >= CAP, 1, 0)
    holder = div(xy, S) == z
    spot = rem(xy, S)

    def w_copy(j):
        return remote(w_send.at[j], w_in.at[spot], wt_s.at[j], wt_r.at[spot], (dp, j))

    def w_arrival(b):
        return remote(w_send.at[b], w_in.at[b], wt_s.at[b], wt_r.at[b], (dp, z * S + b))

    @pl.when(holder)
    def _():
        spread = dot_nn(place[:, c].reshape(NE * PAIR, TOK), prob_ref[...].astype(BF))
        if E < 2 * EL:
            spread = jnp.concatenate(
                [spread, jnp.zeros((NE * PAIR, 2 * EL - E), F32)], axis=1
            )
        spread = jnp.where(slot_lane == slot_expert, spread.reshape(NE, PAIR, 2 * EL), 0.0)
        column = jnp.sum(spread, axis=2, keepdims=True)
        w_send[...] = jnp.broadcast_to(column, (NE, PAIR, 2 * EL)).astype(BF)
        loop(1, NE, lambda k: w_copy(rem(xy + k, NE)).start())
        w_in[spot] = w_send[xy]

    def rs_round(u):
        for k in range(3):
            lag = RS_LAG if k == 2 else 0

            def steps(k=k, lag=lag):
                for r in range(2):
                    rs_step(k, r, u - lag)

            if lag == 0:
                pl.when(u < Z - 2)(steps)
            else:
                pl.when(u >= lag)(steps)

    loop(0, Z - 2 + RS_LAG, rs_round)

    for b in range(S):

        @pl.when(z * S + b != xy)
        def _(b=b):
            w_arrival(b).wait_recv()

    for k in range(3):
        for r in range(2):
            rs_copy(k, r, Z - 2).wait_recv()
    dots = []
    for j in range(2):
        weight = jnp.concatenate(
            [w_in[b].astype(F32)[j * CAP : (j + 1) * CAP, 0:1] for b in range(S)], axis=0
        )
        dot = jnp.zeros((S * CAP, 1), F32)
        for r in range(2):
            both = part[j, r, z].astype(F32) + recv[j, r, Z - 2].astype(F32)
            cols = slice(j * HH, (j + 1) * HH)
            raw = part[2, r, z, :, cols].astype(F32) + recv[2, r, Z - 2, :, cols].astype(F32)
            gate = both[:, 0:HH]
            up = both[:, HH:H]
            sig = 1.0 / (1.0 + jnp.exp(-gate))
            silu = gate * sig
            hidden = silu * up
            d_hidden = raw * weight
            full[j, r, z, :, 0:HH] = (
                d_hidden * up * sig * (1.0 + gate * (1.0 - sig))
            ).astype(BF)
            full[j, r, z, :, HH:H] = (d_hidden * silu).astype(BF)
            full[2, r, z, :, cols] = (hidden * weight).astype(BF)
            dot = dot + jnp.sum(hidden * raw, axis=1, keepdims=True)
            ag_copy(j, r, 0).start()
        dots.append(dot)

    def dots_copy(b):
        return remote(
            dots_send.at[b], dots_in.at[xy], dt_s.at[b], dt_r.at[xy], (dp, z * S + b)
        )

    def dots_arrival(j):
        return remote(dots_send.at[0], dots_in.at[j], dt_s.at[0], dt_r.at[j], (dp, j))

    lane_two = lax.broadcasted_iota(jnp.int32, (PAIR, 2 * EL), 1)
    for b in range(S):
        value = jnp.concatenate(
            [dots[0][b * CAP : (b + 1) * CAP], dots[1][b * CAP : (b + 1) * CAP]], axis=0
        )
        value = jnp.broadcast_to(value, (PAIR, 2 * EL))
        high = value.astype(BF).astype(F32)
        dots_send[b] = jnp.where(lane_two < EL, high, value - high).astype(BF)

        @pl.when(z * S + b != xy)
        def _(b=b):
            dots_copy(b).start()

        @pl.when(z * S + b == xy)
        def _(b=b):
            dots_in[xy] = dots_send[b]

    def ag_round(u):
        for k in range(3):
            lag = AG_LAG if k == 2 else 0

            def steps(k=k, lag=lag):
                for r in range(2):
                    ag_step(k, r, u - lag)

            if lag == 0:
                pl.when(u < Z - 2)(steps)
            else:

                @pl.when(u == lag - 1)
                def _():
                    for r in range(2):
                        ag_copy(2, r, 0).start()

                pl.when(u >= lag)(steps)

    first_stop, second_stop = min(1, Z - 2), min(3, Z - 2)
    loop(0, first_stop, ag_round)

    def top_copy(j):
        return remote(top_send, top_in.at[c], tp_s.at[j], tp_r.at[c], (j, xy))

    def top_arrival(h):
        return remote(
            top_send, top_in.at[h], tp_s.at[h], tp_r.at[h], (div(xy, S) * CORES + h, xy)
        )

    @pl.when(holder)
    def _():
        loop(1, NE, lambda k: dots_arrival(rem(xy + k, NE)).wait_recv())
        lane_e = jnp.where(slot_lane >= EL, slot_lane - EL, slot_lane)
        masked = jnp.where(lane_e == slot_expert, dots_in[...].astype(F32), 0.0).astype(BF)
        top = dot_tn(
            place[:, c].reshape(NE * PAIR, TOK), masked.reshape(NE * PAIR, 2 * EL)
        )
        top_send[...] = top.astype(BF)
        loop(1, ND, lambda k: top_copy(rem(dp + k, ND)).start())
        top_in[c] = top_send[...]

    loop(first_stop, second_stop, ag_round)

    for h in range(CORES):

        @pl.when(div(xy, S) * CORES + h != dp)
        def _(h=h):
            top_arrival(h).wait_recv()

    top = top_in[0].astype(F32) + top_in[1].astype(F32)
    top = top[:, 0:E] + top[:, EL : EL + E]
    mean = sum_out[...].reshape(TOK, 2 * EL)[:, EL : EL + E]
    route = routing[...]
    chosen = jnp.zeros((TOK, E), F32)
    for k in range(route.shape[1]):
        chosen = chosen + jnp.where(route[:, k : k + 1] == lane, 1.0, 0.0)
    d_prob = jnp.where(chosen > 0.5, top, mean)
    prob = prob_ref[...]
    dlogits = prob * (d_prob - jnp.sum(prob * d_prob, axis=1, keepdims=True))
    high, low = split_two(dlogits)
    dlog_hi[...] = high
    dlog_lo[...] = low
    router_part = dot_tn(tokens[...], high) + dot_tn(tokens[...], low)
    gr_src[...] = packed(router_part[0:TOK], router_part[TOK : 2 * TOK], NE)
    p2_send()

    loop(second_stop, Z - 2, ag_round)
    p2_reduce()

    for k in range(2):
        for r in range(2):
            ag_arrival(k, r, Z - 2).wait_recv()

    for j in range(2):
        total = None
        for r in range(2):
            cols = slice(r * HH, (r + 1) * HH)
            both = full[j, r].reshape(ROWS, H)
            term = dot_nt(both[:, 0:HH], wg[j, :, cols]) + dot_nt(both[:, HH:H], wu[j, :, cols])
            total = term if total is None else total + term
        dx_ref[j] = total

    def back_copy(q2):
        return remote(
            back_send.at[div(q2, CORES), rem(q2, CORES)], back_in.at[q],
            bk_s.at[q2], bk_r.at[q], plane_peer(q2),
        )

    def back_arrival(q2):
        return remote(
            back_send.at[div(q2, CORES), rem(q2, CORES)], back_in.at[q2],
            bk_s.at[q2], bk_r.at[q2], plane_peer(q2),
        )

    def order_back(i):
        at = pl.ds(pl.multiple_of(i * CAP, CAP), CAP)
        block = jnp.concatenate([dx_ref[0, at, :], dx_ref[1, at, :]], axis=0).astype(BF)
        for h in range(CORES):
            back_send[i, h] = block[:, h * W : (h + 1) * W]

    loop(0, NE, order_back)
    loop(1, NQ, lambda k: back_copy(rem(q + k, NQ)).start())
    back_in[q] = back_send[xy, c]

    loop(Z - 2, Z - 2 + AG_LAG, ag_round)

    def out_copies(i, j):
        expert = c * 2 + j
        out = (grad_gate, grad_up, grad_down)[i]
        buf = (out_gate, out_up, out_down)[i]
        if i < 2:
            keep, give = buf.at[j, half, :], buf.at[j, other_half, :]
        else:
            keep, give = buf.at[c, j], buf.at[other, j]
        local = pltpu.make_async_copy(keep, out.at[expert], ol_s.at[i, j])
        send = remote(give, out.at[expert], ox_s.at[i, j], ox_r.at[i, j], twin)
        arrival = remote(give, out.at[other * 2 + j], ox_s.at[i, j], ox_r.at[i, j], twin)
        return local, send, arrival

    for j in range(2):
        for r in range(2):
            cols = slice(r * HH, (r + 1) * HH)
            both = full[j, r].reshape(ROWS, H)
            out_gate[j, :, cols] = dot_tn(rows[0, j], both[:, 0:HH]).astype(BF)
            out_up[j, :, cols] = dot_tn(rows[0, j], both[:, HH:H]).astype(BF)
        for i in range(2):
            local, send, _ = out_copies(i, j)
            send.start()
            local.start()

    for r in range(2):
        ag_arrival(2, r, Z - 2).wait_recv()
    for j in range(2):
        for r in range(2):
            units = slice(r * HH, (r + 1) * HH)
            hid = full[2, r, :, :, j * HH : (j + 1) * HH].reshape(ROWS, HH)
            value = dot_tn(hid, rows[1, j]).astype(BF)
            out_down[0, j, units, :] = value[:, 0:W]
            out_down[1, j, units, :] = value[:, W : 2 * W]
        local, send, _ = out_copies(2, j)
        send.start()
        local.start()

    p2_finish()
    packed_sum = gr_out[...].reshape(TOK, 2 * EL)
    grad_router[0:TOK, :] = packed_sum[:, 0:E]
    grad_router[TOK : 2 * TOK, :] = packed_sum[:, EL : EL + E]
    loop(1, NQ, lambda k: back_arrival(rem(q + k, NQ)).wait_recv())
    router_term = dot_nt(dlog_hi[...], w_router[...]) + dot_nt(dlog_lo[...], w_router[...])
    token_term = dot_tn(
        place[...].reshape(E * CAP, TOK), back_in[...].reshape(E * CAP, W)
    )
    grad_tokens[...] = (token_term + router_term).astype(BF)

    loop(1, NQ, lambda k: rows_copy(0, rem(q + k, NQ)).wait_send())
    loop(1, NQ, lambda k: rows_copy(1, rem(q + k, NQ)).wait_send())
    loop(1, NQ, lambda k: back_copy(rem(q + k, NQ)).wait_send())
    for copy in weight_copies:
        copy.wait_send()
    p1_drain()
    p2_drain()

    def ring_drain(s):
        for k in range(3):
            for r in range(2):
                rs_copy(k, r, s).wait_send()
                ag_copy(k, r, s).wait_send()

    loop(0, Z - 1, ring_drain)

    @pl.when(holder)
    def _():
        loop(1, NE, lambda k: w_copy(rem(xy + k, NE)).wait_send())
        loop(1, ND, lambda k: top_copy(rem(dp + k, ND)).wait_send())

    for b in range(S):

        @pl.when(z * S + b != xy)
        def _(b=b):
            dots_copy(b).wait_send()

    for i in range(3):
        for j in range(2):
            local, send, arrival = out_copies(i, j)
            local.wait()
            send.wait_send()
            arrival.wait_recv()


def per_device(tokens, cotangent, routing, w_router, running_mean, w_gate, w_up, w_down):
    NE = lax.axis_size("expert")
    ND = lax.axis_size("dp")
    Z = ND // CORES
    local_count, W, H = w_gate.shape
    E = NE * local_count
    TOK, top = routing.shape
    CAP = 3 * TOK * top // (2 * E)
    NQ = NE * CORES
    S = NE // Z
    PAIR, ROWS, HH = 2 * CAP, NE * CAP, H // 2
    sizes = (NE, Z, E, TOK, H, W, CAP)
    vmem = pl.BlockSpec(memory_space=pltpu.VMEM)
    hbm = pl.BlockSpec(memory_space=pl.ANY)
    dma = pltpu.SemaphoreType.DMA
    scratch = [
        pltpu.VMEM((NE, CORES, PAIR, TOK), BF),
        pltpu.VMEM((2, NQ, PAIR, W), BF),
        pltpu.VMEM((2, CORES, NE, PAIR, W), BF),
        pltpu.VMEM((2, 2, ROWS, 2 * W), BF),
        pltpu.VMEM((2, 2 * W, H), BF),
        pltpu.VMEM((2, 2 * W, H), BF),
        pltpu.VMEM((2, 2, H, W), BF),
        pltpu.VMEM((3, 2, Z, S * CAP, H), BF),
        pltpu.VMEM((3, 2, Z - 1, S * CAP, H), BF),
        pltpu.VMEM((3, 2, Z, S * CAP, H), BF),
        pltpu.VMEM((ND, TOK // ND, 128), F32),
        pltpu.VMEM((ND, TOK // ND, 128), F32),
        pltpu.VMEM((ND, TOK // ND, 128), F32),
        pltpu.VMEM((NE, TOK // NE, 128), F32),
        pltpu.VMEM((NE, TOK // NE, 128), F32),
        pltpu.VMEM((NE, TOK // NE, 128), F32),
        pltpu.VMEM((TOK, E), F32),
        pltpu.VMEM((NE, PAIR, 128), BF),
        pltpu.VMEM((S, PAIR, 128), BF),
        pltpu.VMEM((S, PAIR, 128), BF),
        pltpu.VMEM((NE, PAIR, 128), BF),
        pltpu.VMEM((TOK, 128), BF),
        pltpu.VMEM((2, TOK, 128), BF),
        pltpu.VMEM((TOK, E), BF),
        pltpu.VMEM((TOK, E), BF),
        pltpu.VMEM((2, ROWS, 2 * W), F32),
        pltpu.VMEM((NE, CORES, PAIR, W), BF),
        pltpu.VMEM((NQ, PAIR, W), BF),
        pltpu.VMEM((2, 2 * W, H), BF),
        pltpu.VMEM((2, 2 * W, H), BF),
        pltpu.VMEM((2, 2, H, W), BF),
        dma((2, NQ)), dma((2, NQ)),
        dma((3,)), dma((3,)), dma((3,)),
        dma((2, ND)), dma((2, ND)),
        dma((2, NE)), dma((2, NE)),
        dma((3, 2, Z - 1)), dma((3, 2, Z - 1)),
        dma((3, 2, Z - 1)), dma((3, 2, Z - 1)),
        dma((NE,)), dma((S,)),
        dma((S,)), dma((NE,)),
        dma((ND,)), dma((2,)),
        dma((NQ,)), dma((NQ,)),
        dma((3, 2)), dma((3, 2)), dma((3, 2)),
    ]
    return pl.pallas_call(
        functools.partial(kernel, sizes),
        out_shape=(
            jax.ShapeDtypeStruct((TOK, W), BF),
            jax.ShapeDtypeStruct((W, E), F32),
            jax.ShapeDtypeStruct((local_count, W, H), BF),
            jax.ShapeDtypeStruct((local_count, W, H), BF),
            jax.ShapeDtypeStruct((local_count, H, W), BF),
        ),
        in_specs=[vmem] * 5 + [hbm] * 3,
        out_specs=(vmem, vmem, hbm, hbm, hbm),
        scratch_shapes=scratch,
        compiler_params=pltpu.CompilerParams(
            collective_id=0, has_side_effects=True, vmem_limit_bytes=56 * 1024 * 1024
        ),
        cost_estimate=pl.CostEstimate(
            flops=6 * 10**9, bytes_accessed=10**7, transcendentals=10**5
        ),
    )(tokens, cotangent, routing, w_router, running_mean, w_gate, w_up, w_down)


def solution(mesh):
    return jax.shard_map(
        per_device,
        mesh=mesh,
        in_specs=(
            P("expert", "dp"),
            P("expert", "dp"),
            P("expert", None),
            P("dp", None),
            P(None, "dp"),
            P("expert", "dp", None),
            P("expert", "dp", None),
            P("expert", None, "dp"),
        ),
        out_specs=(
            P("expert", "dp"),
            P("dp", None),
            P("expert", "dp", None),
            P("expert", "dp", None),
            P("expert", None, "dp"),
        ),
        check_vma=False,
    )
```

time: 449 us -> 145 us (0.32)
  waiting for transfers between devices: 205 us -> 0 us
  Pallas kernels: 0 us -> 132 us
  blocking collectives: 126 us -> 0 us
  matrix products: 35.5 us -> 0 us
  other arithmetic: 35.5 us -> 0 us
  starting transfers between devices: 20.3 us -> 0 us
  between operations: 14 us -> 0.64 us
    psum x3 -> x0, waiting for transfers between devices: 192 us -> none  [the longest x1 65.8 us: per_device(): grad_router = lax.psum(router_part, 'expert')]
    pallas_call x0 -> x1, Pallas kernels: none -> 132 us  [per_device(): pl.pallas_call(functools.partial(kernel, sizes), out_shape=(jax.ShapeDtyp...]
    psum x2 -> x0, blocking collectives: 95.6 us -> none  [the longest x1 49.9 us: per_device(): logits = lax.psum(partial_logits, 'dp')]
    dot_general x18 -> x0, matrix products: 35.5 us -> none  [the longest x1 7.07 us: per_device(): jnp.dot(select_float, back_dots, precision=lax.Precision.HIGHEST)]
    all_to_all x2 -> x0, blocking collectives: 30.8 us -> none  [the longest x1 20.2 us: per_device(): lax.all_to_all(send_rows, 'expert', split_axis=0, concat_axis=0, tiled=True)]
    all_to_all x3 -> x0, starting transfers between devices: 20 us -> none  [the longest x1 7.29 us: per_device(): lax.all_to_all(dx_slots, 'expert', split_axis=0, concat_axis=0, tiled=True)]
    another operation x3 -> x0, other arithmetic: 18.2 us -> none
    all_to_all x3 -> x0, waiting for transfers between devices: 12.6 us -> none  [the longest x1 6.65 us: per_device(): lax.all_to_all(dx_slots, 'expert', split_axis=0, concat_axis=0, tiled=True)]
  transfers between devices with their start and end apart: 6 -> 0, of which waited for: 5 -> 0; matrix products, arithmetic and copies ran while one was open for 7% -> 0% of each run, Pallas kernels for 0% -> 0%
where the time goes in v1:
time: 145 us; the launch traced here: 144 us
  Pallas kernels  132 us (91%)
  local copies, waits for them, and re-layouts  11.9 us (8%)
    pallas_call x1, Pallas kernels, per_device(): pl.pallas_call(functools.partial(kernel, sizes), out_shape=(jax.ShapeDtyp...  132 us
    unnamed x10, local copies, waits for them, and re-layouts  10.3 us

profile of v1, /device:TPU:2, one launch (start us, length us, event | category | flops | bytes accessed | tf_op | source)
XLA Modules:
  0.0 144.3 jit_solution(2227035339769250365)
XLA Ops:
  0.6 1.4 copy.13.routing
  2.0 1.5 %copy.14.w_router = bf16[256,64]{1,0:T(8,128)(2,1)} copy(bf16[256,64]{0,1:T(8,128)(2,1)} %param.11) | data formatting | bytes 65536 | tf_op args[3]
  3.5 131.8 %shard_map.119 = (bf16[128,256]{1,0:T(8,128)(2,1)}, f32[256,64]{1,0:T(8,128)}, bf16[4,256,768]{2,1,0:T(8,128)(2,1)}, bf16[4,256,768]{2,1,0:T(8,128)(2,1)}, bf16[4,768,256]{2,1,0:T(8,128)(2,1)}) custom-call(bf16[128,256]{1,0:T(8,128)(2,1)} %tokens.1, bf16[128,256]{1,0:T(8,128)(2,1)} %cotangent.1, s32[128,8]{1,0:T(8,128)} %copy.13.routing, ...), custom_call_target="tpu_custom_call" | custom-call | flops 6000000000 | bytes 10000000 | tf_op jit(solution)/shard_map/pallas_call | solution.py:664
  135.3 1.6 %copy.15 = f32[256,64]{0,1:T(8,128)} copy(f32[256,64]{1,0:T(8,128)} %get-tuple-element.6) | data formatting | bytes 131072 | tf_op jit(solution)/shard_map/pallas_call | solution.py:664
  136.9 1.5 %copy.20 = bf16[128,256]{1,0:T(8,128)(2,1)} copy(bf16[128,256]{1,0:T(8,128)(2,1)} %get-tuple-element.15) | data formatting | bytes 131072
  138.4 0.0 copy-start.1
  138.4 2.8 %copy.21 = bf16[4,256,768]{2,1,0:T(8,128)(2,1)} copy(bf16[4,256,768]{2,1,0:T(8,128)(2,1)} %get-tuple-element.17) | data formatting | bytes 3145728
  141.2 0.0 copy-done.1
  141.2 0.0 copy-start
  141.2 1.1 copy.22
  142.3 0.8 copy-done
  143.2 1.1 copy.23
Async XLA Ops:
  138.4 2.8 %copy-start.1 = (bf16[4,256,768]{2,1,0:T(8,128)(2,1)S(1)}, bf16[4,256,768]{2,1,0:T(8,128)(2,1)}, u32[]{:S(2)}) copy-start(bf16[4,256,768]{2,1,0:T(8,128)(2,1)} %get-tuple-element.18) | copy-start | bytes 4718596
  141.2 2.0 %copy-start = (bf16[4,768,256]{2,1,0:T(8,128)(2,1)S(1)}, bf16[4,768,256]{2,1,0:T(8,128)(2,1)}, u32[]{:S(2)}) copy-start(bf16[4,768,256]{2,1,0:T(8,128)(2,1)} %get-tuple-element.19) | copy-start | bytes 4718596

commit v2 on v1

--- a/solution.py
+++ b/solution.py
@@ -11,7 +11,7 @@
 BF = jnp.bfloat16
 F32 = jnp.float32
 CORES = 2
-RS_LAG = 2
+RS_LAG = 3
 AG_LAG = 3
 
 
@@ -67,7 +67,7 @@
     place, send_rows, in_rows, rows, wg, wu, wd,
     part, recv, full,
     sum_src, sum_in, sum_out, gr_src, gr_in, gr_out,
-    prob_ref, w_send, w_in, dots_send, dots_in, top_send, top_in, dlog_hi, dlog_lo,
+    prob_ref, chosen_ref, w_send, w_in, dots_send, dots_in, top_send, top_in, dlog_hi, dlog_lo,
     dx_ref, back_send, back_in, out_gate, out_up, out_down,
     rows_s, rows_r, wx_s, wx_r, wl_s,
     p1_s, p1_r, p2_s, p2_r,
@@ -81,6 +81,7 @@
     S = NE // Z
     HH = H // 2
     EL = 64
+    GB = NE // (W // 128)
     PAIR = 2 * CAP
     ROWS = NE * CAP
 
@@ -96,6 +97,22 @@
 
     def plane_peer(q2):
         return (z * CORES + rem(q2, CORES), div(q2, CORES))
+
+    side = 4 if NE % 4 == 0 else NE
+
+    def ahead(k):
+        a, rest = rem(k, side), div(k, side)
+        b, d = rem(rest, NE // side), div(rest, NE // side)
+        x2 = rem(rem(xy, side) + a, side)
+        y2 = rem(div(xy, side) + b, NE // side)
+        return (y2 * side + x2) * CORES + rem(c + d, CORES)
+
+    def behind(k):
+        a, rest = rem(k, side), div(k, side)
+        b, d = rem(rest, NE // side), div(rest, NE // side)
+        x2 = rem(rem(xy, side) + side - a, side)
+        y2 = rem(div(xy, side) + NE // side - b, NE // side)
+        return (y2 * side + x2) * CORES + rem(c + CORES - d, CORES)
 
     barrier = pltpu.get_barrier_semaphore()
 
@@ -128,18 +145,16 @@
         copy.start()
 
     route = routing[...]
-    lane = lax.broadcasted_iota(jnp.int32, (TOK, E), 1)
-    chosen = jnp.zeros((TOK, E), F32)
-    for k in range(route.shape[1]):
-        chosen = chosen + jnp.where(route[:, k : k + 1] == lane, 1.0, 0.0)
-    chosen_b = chosen.astype(BF)
+    row_e = lax.broadcasted_iota(jnp.int32, (E, TOK), 0)
+    has = jnp.zeros((E, TOK), F32)
+    for k in range(route.shape[0]):
+        has = has + jnp.where(route[k : k + 1, :] == row_e, 1.0, 0.0)
     t_row = lax.broadcasted_iota(jnp.int32, (TOK, TOK), 0)
     t_col = lax.broadcasted_iota(jnp.int32, (TOK, TOK), 1)
     before = jnp.where(t_row < t_col, 1.0, 0.0).astype(BF)
     same = jnp.where(t_row == t_col, 1.0, 0.0).astype(BF)
-    pos = dot_tn(chosen_b, before)
-    has = dot_tn(chosen_b, same)
-    pos = jnp.where(has > 0.5, pos, -1.0)
+    pos = jnp.where(has > 0.5, dot_nn(has.astype(BF), before), -1.0)
+    chosen_ref[...] = dot_nt(same, has.astype(BF))
     slot_iota = lax.broadcasted_iota(jnp.int32, (E, CAP, TOK), 1).astype(F32)
     placing = jnp.where(pos[:, None, :] == slot_iota, 1.0, 0.0)
     placing = placing.reshape(E * CAP, TOK).astype(BF)
@@ -174,9 +189,7 @@
     ]
     weight_copies[0].start()
     weight_copies[1].start()
-    loop(1, NQ, lambda k: rows_copy(0, rem(q + k, NQ)).start())
-    loop(1, NQ, lambda k: rows_copy(1, rem(q + k, NQ)).start())
-    weight_copies[2].start()
+    loop(1, NQ, lambda k: rows_copy(0, ahead(k)).start())
     in_rows[0, c, xy] = send_rows[0, q]
     in_rows[1, c, xy] = send_rows[1, q]
 
@@ -227,7 +240,7 @@
             second = jnp.concatenate([second, gap], axis=1)
         return jnp.concatenate([first, second], axis=1).reshape(count, TOK // count, 2 * EL)
 
-    logits_part = dot_nn(tokens[...], w_router[...])
+    logits_part = dot_nt(tokens[...], w_router[...])
     mean_part = dot_nt(cotangent[...], running_mean[...])
     sum_src[...] = packed(logits_part, mean_part, ND)
     p1_send()
@@ -279,7 +292,12 @@
     own_copies[1].wait()
     weight_arrivals[0].wait_recv()
     weight_arrivals[1].wait_recv()
-    loop(1, NQ, lambda k: rows_arrival(0, rem(q + k, NQ)).wait_recv())
+    def rows_then_grads(k):
+        rows_arrival(0, behind(k)).wait_recv()
+        rows_copy(1, ahead(k)).start()
+
+    loop(1, NQ, rows_then_grads)
+    weight_copies[2].start()
     order_rows(0)
     for j in range(2):
         for r in range(2):
@@ -293,6 +311,21 @@
             rs_copy(j, r, 0).start()
 
     p1_reduce()
+
+    def rs_round(u):
+        for k in range(3):
+            lag = RS_LAG if k == 2 else 0
+
+            def steps(k=k, lag=lag):
+                for r in range(2):
+                    rs_step(k, r, u - lag)
+
+            if lag == 0:
+                pl.when(u < Z - 2)(steps)
+            else:
+                pl.when(u >= lag)(steps)
+
+    loop(0, RS_LAG, rs_round)
 
     own_copies[2].wait()
     weight_arrivals[2].wait_recv()
@@ -338,20 +371,7 @@
         loop(1, NE, lambda k: w_copy(rem(xy + k, NE)).start())
         w_in[spot] = w_send[xy]
 
-    def rs_round(u):
-        for k in range(3):
-            lag = RS_LAG if k == 2 else 0
-
-            def steps(k=k, lag=lag):
-                for r in range(2):
-                    rs_step(k, r, u - lag)
-
-            if lag == 0:
-                pl.when(u < Z - 2)(steps)
-            else:
-                pl.when(u >= lag)(steps)
-
-    loop(0, Z - 2 + RS_LAG, rs_round)
+    loop(RS_LAG, Z - 2 + RS_LAG, rs_round)
 
     for b in range(S):
 
@@ -431,56 +451,7 @@
 
                 pl.when(u >= lag)(steps)
 
-    first_stop, second_stop = min(1, Z - 2), min(3, Z - 2)
-    loop(0, first_stop, ag_round)
-
-    def top_copy(j):
-        return remote(top_send, top_in.at[c], tp_s.at[j], tp_r.at[c], (j, xy))
-
-    def top_arrival(h):
-        return remote(
-            top_send, top_in.at[h], tp_s.at[h], tp_r.at[h], (div(xy, S) * CORES + h, xy)
-        )
-
-    @pl.when(holder)
-    def _():
-        loop(1, NE, lambda k: dots_arrival(rem(xy + k, NE)).wait_recv())
-        lane_e = jnp.where(slot_lane >= EL, slot_lane - EL, slot_lane)
-        masked = jnp.where(lane_e == slot_expert, dots_in[...].astype(F32), 0.0).astype(BF)
-        top = dot_tn(
-            place[:, c].reshape(NE * PAIR, TOK), masked.reshape(NE * PAIR, 2 * EL)
-        )
-        top_send[...] = top.astype(BF)
-        loop(1, ND, lambda k: top_copy(rem(dp + k, ND)).start())
-        top_in[c] = top_send[...]
-
-    loop(first_stop, second_stop, ag_round)
-
-    for h in range(CORES):
-
-        @pl.when(div(xy, S) * CORES + h != dp)
-        def _(h=h):
-            top_arrival(h).wait_recv()
-
-    top = top_in[0].astype(F32) + top_in[1].astype(F32)
-    top = top[:, 0:E] + top[:, EL : EL + E]
-    mean = sum_out[...].reshape(TOK, 2 * EL)[:, EL : EL + E]
-    route = routing[...]
-    chosen = jnp.zeros((TOK, E), F32)
-    for k in range(route.shape[1]):
-        chosen = chosen + jnp.where(route[:, k : k + 1] == lane, 1.0, 0.0)
-    d_prob = jnp.where(chosen > 0.5, top, mean)
-    prob = prob_ref[...]
-    dlogits = prob * (d_prob - jnp.sum(prob * d_prob, axis=1, keepdims=True))
-    high, low = split_two(dlogits)
-    dlog_hi[...] = high
-    dlog_lo[...] = low
-    router_part = dot_tn(tokens[...], high) + dot_tn(tokens[...], low)
-    gr_src[...] = packed(router_part[0:TOK], router_part[TOK : 2 * TOK], NE)
-    p2_send()
-
-    loop(second_stop, Z - 2, ag_round)
-    p2_reduce()
+    loop(0, Z - 2, ag_round)
 
     for k in range(2):
         for r in range(2):
@@ -514,8 +485,28 @@
             back_send[i, h] = block[:, h * W : (h + 1) * W]
 
     loop(0, NE, order_back)
-    loop(1, NQ, lambda k: back_copy(rem(q + k, NQ)).start())
+    loop(1, NQ, lambda k: back_copy(ahead(k)).start())
     back_in[q] = back_send[xy, c]
+
+    def top_copy(j):
+        return remote(top_send, top_in.at[c], tp_s.at[j], tp_r.at[c], (j, xy))
+
+    def top_arrival(h):
+        return remote(
+            top_send, top_in.at[h], tp_s.at[h], tp_r.at[h], (div(xy, S) * CORES + h, xy)
+        )
+
+    @pl.when(holder)
+    def _():
+        loop(1, NE, lambda k: dots_arrival(rem(xy + k, NE)).wait_recv())
+        lane_e = jnp.where(slot_lane >= EL, slot_lane - EL, slot_lane)
+        masked = jnp.where(lane_e == slot_expert, dots_in[...].astype(F32), 0.0).astype(BF)
+        top = dot_tn(
+            place[:, c].reshape(NE * PAIR, TOK), masked.reshape(NE * PAIR, 2 * EL)
+        )
+        top_send[...] = top.astype(BF)
+        loop(1, ND, lambda k: top_copy(rem(dp + k, ND)).start())
+        top_in[c] = top_send[...]
 
     loop(Z - 2, Z - 2 + AG_LAG, ag_round)
 
@@ -543,6 +534,28 @@
             send.start()
             local.start()
 
+    for h in range(CORES):
+
+        @pl.when(div(xy, S) * CORES + h != dp)
+        def _(h=h):
+            top_arrival(h).wait_recv()
+
+    top = top_in[0].astype(F32) + top_in[1].astype(F32)
+    top = top[:, 0:E] + top[:, EL : EL + E]
+    mean = sum_out[...].reshape(TOK, 2 * EL)[:, EL : EL + E]
+    d_prob = jnp.where(chosen_ref[...] > 0.5, top, mean)
+    prob = prob_ref[...]
+    dlogits = prob * (d_prob - jnp.sum(prob * d_prob, axis=1, keepdims=True))
+    high, low = split_two(dlogits)
+    dlog_hi[...] = high
+    dlog_lo[...] = low
+    router_part = dot_tn(high, tokens[...]) + dot_tn(low, tokens[...])
+    for h in range(W // 128):
+        gr_src[h * GB : (h + 1) * GB] = router_part[:, h * 128 : (h + 1) * 128].reshape(
+            GB, E // GB, 128
+        )
+    p2_send()
+
     for r in range(2):
         ag_arrival(2, r, Z - 2).wait_recv()
     for j in range(2):
@@ -556,16 +569,16 @@
         send.start()
         local.start()
 
-    p2_finish()
-    packed_sum = gr_out[...].reshape(TOK, 2 * EL)
-    grad_router[0:TOK, :] = packed_sum[:, 0:E]
-    grad_router[TOK : 2 * TOK, :] = packed_sum[:, EL : EL + E]
+    p2_reduce()
     loop(1, NQ, lambda k: back_arrival(rem(q + k, NQ)).wait_recv())
-    router_term = dot_nt(dlog_hi[...], w_router[...]) + dot_nt(dlog_lo[...], w_router[...])
+    router_term = dot_nn(dlog_hi[...], w_router[...]) + dot_nn(dlog_lo[...], w_router[...])
     token_term = dot_tn(
         place[...].reshape(E * CAP, TOK), back_in[...].reshape(E * CAP, W)
     )
     grad_tokens[...] = (token_term + router_term).astype(BF)
+    p2_finish()
+    for h in range(W // 128):
+        grad_router[:, h * 128 : (h + 1) * 128] = gr_out[h * GB : (h + 1) * GB].reshape(E, 128)
 
     loop(1, NQ, lambda k: rows_copy(0, rem(q + k, NQ)).wait_send())
     loop(1, NQ, lambda k: rows_copy(1, rem(q + k, NQ)).wait_send())
@@ -602,6 +615,17 @@
             arrival.wait_recv()
 
 
+def write_out(*refs):
+    sources, targets, sems = refs[:5], refs[5:10], refs[10]
+    copies = [
+        pltpu.make_async_copy(sources[i], targets[i], sems.at[i]) for i in (2, 3, 4, 0, 1)
+    ]
+    for copy in copies:
+        copy.start()
+    for copy in copies:
+        copy.wait()
+
+
 def per_device(tokens, cotangent, routing, w_router, running_mean, w_gate, w_up, w_down):
     NE = lax.axis_size("expert")
     ND = lax.axis_size("dp")
@@ -609,6 +633,7 @@
     local_count, W, H = w_gate.shape
     E = NE * local_count
     TOK, top = routing.shape
+    routing, w_router = routing.T, w_router.T
     CAP = 3 * TOK * top // (2 * E)
     NQ = NE * CORES
     S = NE // Z
@@ -631,9 +656,10 @@
         pltpu.VMEM((ND, TOK // ND, 128), F32),
         pltpu.VMEM((ND, TOK // ND, 128), F32),
         pltpu.VMEM((ND, TOK // ND, 128), F32),
-        pltpu.VMEM((NE, TOK // NE, 128), F32),
-        pltpu.VMEM((NE, TOK // NE, 128), F32),
-        pltpu.VMEM((NE, TOK // NE, 128), F32),
+        pltpu.VMEM((NE, E * W // (128 * NE), 128), F32),
+        pltpu.VMEM((NE, E * W // (128 * NE), 128), F32),
+        pltpu.VMEM((NE, E * W // (128 * NE), 128), F32),
+        pltpu.VMEM((TOK, E), F32),
         pltpu.VMEM((TOK, E), F32),
         pltpu.VMEM((NE, PAIR, 128), BF),
         pltpu.VMEM((S, PAIR, 128), BF),
@@ -661,17 +687,17 @@
         dma((NQ,)), dma((NQ,)),
         dma((3, 2)), dma((3, 2)), dma((3, 2)),
     ]
-    return pl.pallas_call(
+    results = pl.pallas_call(
         functools.partial(kernel, sizes),
         out_shape=(
-            jax.ShapeDtypeStruct((TOK, W), BF),
-            jax.ShapeDtypeStruct((W, E), F32),
-            jax.ShapeDtypeStruct((local_count, W, H), BF),
-            jax.ShapeDtypeStruct((local_count, W, H), BF),
-            jax.ShapeDtypeStruct((local_count, H, W), BF),
+            pltpu.VMEM((TOK, W), BF),
+            pltpu.VMEM((E, W), F32),
+            pltpu.VMEM((local_count, W, H), BF),
+            pltpu.VMEM((local_count, W, H), BF),
+            pltpu.VMEM((local_count, H, W), BF),
         ),
         in_specs=[vmem] * 5 + [hbm] * 3,
-        out_specs=(vmem, vmem, hbm, hbm, hbm),
+        out_specs=(vmem, vmem, vmem, vmem, vmem),
         scratch_shapes=scratch,
         compiler_params=pltpu.CompilerParams(
             collective_id=0, has_side_effects=True, vmem_limit_bytes=56 * 1024 * 1024
@@ -680,6 +706,14 @@
             flops=6 * 10**9, bytes_accessed=10**7, transcendentals=10**5
         ),
     )(tokens, cotangent, routing, w_router, running_mean, w_gate, w_up, w_down)
+    grad_tokens, grad_router, *rest = pl.pallas_call(
+        write_out,
+        out_shape=[jax.ShapeDtypeStruct(x.shape, x.dtype) for x in results],
+        in_specs=[hbm] * 5,
+        out_specs=[hbm] * 5,
+        scratch_shapes=[dma((5,))],
+    )(*results)
+    return (grad_tokens, grad_router.T, *rest)
 
 
 def solution(mesh):

time: 145 us -> 287 us (1.98)
  Pallas kernels: 132 us -> 281 us
  local copies, waits for them, and re-layouts: 11.9 us -> 4.71 us
    pallas_call x1 -> x2, Pallas kernels: 132 us -> 281 us  [the longest x1 148 us: per_device(): pl.pallas_call(write_out, out_shape=[jax.ShapeDtypeStruct(x.shape, x.dtyp...]
    unnamed x10, local copies, waits for them, and re-layouts: 10.3 us -> 4.71 us
where the time goes in v2:
time: 287 us
  Pallas kernels  281 us (98%)
  local copies, waits for them, and re-layouts  4.71 us (2%)
    pallas_call x1, Pallas kernels, per_device(): pl.pallas_call(write_out, out_shape=[jax.ShapeDtypeStruct(x.shape, x.dtyp...  148 us
    pallas_call x1, Pallas kernels, per_device(): pl.pallas_call(functools.partial(kernel, sizes), out_shape=(pltpu.VMEM((T...  133 us

profile of v2, /device:TPU:2, one launch (start us, length us, event | category | flops | bytes accessed | tf_op | source)
XLA Modules:
  0.0 286.7 jit_solution(4577794715987372339)
XLA Ops:
  0.6 133.3 %shard_map.119 = (bf16[128,256]{1,0:T(8,128)(2,1)S(1)}, f32[64,256]{1,0:T(8,128)S(1)}, bf16[4,256,768]{2,1,0:T(8,128)(2,1)S(1)}, bf16[4,256,768]{2,1,0:T(8,128)(2,1)S(1)}, bf16[4,768,256]{2,1,0:T(8,128)(2,1)S(1)}) custom-call(bf16[128,256]{1,0:T(8,128)(2,1)} %tokens.1, bf16[128,256]{1,0:T(8,128)(2,1)} %cotangent.1, s32[8,128]{1,0:T(8,128)} %bitcast.5, ...), custom_call_target="tpu_custom_call" | custom-call | flops 6000000000 | bytes 10000000 | tf_op jit(solution)/shard_map/pallas_call | solution.py:690
  133.9 0.0 copy-start
  133.9 1.1 copy-done
  135.1 0.0 copy-start.1
  135.1 1.2 copy-done.1
  136.2 0.0 copy-start.2
  136.2 1.2 copy-done.2
  137.4 0.0 copy-start.3
  137.4 0.6 copy-done.3
  138.0 0.0 copy-start.4
  138.0 0.6 copy-done.4
  138.6 148.1 %shard_map.120 = (bf16[128,256]{1,0:T(8,128)(2,1)}, f32[64,256]{1,0:T(8,128)}, bf16[4,256,768]{2,1,0:T(8,128)(2,1)}, bf16[4,256,768]{2,1,0:T(8,128)(2,1)}, bf16[4,768,256]{2,1,0:T(8,128)(2,1)}) custom-call(bf16[128,256]{1,0:T(8,128)(2,1)} %copy-done.3, f32[64,256]{1,0:T(8,128)} %copy-done.4, bf16[4,256,768]{2,1,0:T(8,128)(2,1)} %copy-done, ...), custom_call_target="tpu_custom_call" | custom-call | tf_op jit(solution)/shard_map/pallas_call | solution.py:709
Async XLA Ops:
  133.9 1.2 copy-start
  135.1 1.2 copy-start.1
  136.2 1.2 copy-start.2
  137.4 0.6 copy-start.3
  138.0 0.6 copy-start.4

commit v3 on v2

v3 whole, which is shorter than its diff:
```python
import functools

import jax
import jax.numpy as jnp
from jax import lax
from jax.experimental import pallas as pl
from jax.experimental.pallas import tpu as pltpu
from jax.sharding import PartitionSpec as P

MESH = pl.DeviceIdType.MESH
BF = jnp.bfloat16
F32 = jnp.float32
CORES = 2
ROWS_FIRST = 3
GRADS_FIRST = 0
GRADS_NEXT = 4


def rem(a, n):
    return lax.rem(a, jnp.int32(n))


def div(a, n):
    return lax.div(a, jnp.int32(n))


def remote(src, dst, send_sem, recv_sem, device):
    return pltpu.make_async_remote_copy(
        src_ref=src,
        dst_ref=dst,
        send_sem=send_sem,
        recv_sem=recv_sem,
        device_id=device,
        device_id_type=MESH,
    )


def loop(lower, upper, body):
    def step(i, carry):
        body(i)
        return carry

    lax.fori_loop(lower, upper, step, 0)


def dot_nn(a, b):
    return jnp.dot(a, b, preferred_element_type=F32)


def dot_nt(a, b):
    return lax.dot_general(a, b, (((1,), (1,)), ((), ())), preferred_element_type=F32)


def dot_tn(a, b):
    return lax.dot_general(a, b, (((0,), (0,)), ((), ())), preferred_element_type=F32)


def split_two(value):
    high = value.astype(BF)
    low = (value - high.astype(F32)).astype(BF)
    return high, low


def kernel(
    sizes,
    tokens, cotangent, routing, w_router, running_mean, w_gate, w_up, w_down,
    grad_tokens, grad_router, grad_gate, grad_up, grad_down,
    place, send_rows, in_rows, rows, wg, wu, wd,
    part, recv, full,
    sum_src, sum_in, sum_out, gr_src, gr_in, gr_out,
    top_src, top_parts, top_out,
    prob_ref, chosen_ref, w_send, w_in, dots_send, dots_in, dlog_hi, dlog_lo,
    back_send, back_in, out_gate, out_up, out_down,
    rows_s, rows_r, wx_s, wx_r, wl_s,
    p1_s, p1_r, p2_s, p2_r, p3_s, p3_r,
    rs_s, rs_r, ag_s, ag_r,
    wt_s, wt_r, dt_s, dt_r, bk_s, bk_r,
    ox_s, ox_r,
):
    NE, Z, E, TOK, H, W, CAP = sizes
    ND = Z * CORES
    NQ = NE * CORES
    S = NE // Z
    HZ = Z // 2
    HH = H // 2
    SC = S * CAP
    EL = 64
    GB = NE // (W // 128)
    PAIR = 2 * CAP
    ROWS = NE * CAP

    dp = lax.axis_index("dp")
    xy = lax.axis_index("expert")
    z = div(dp, CORES)
    c = rem(dp, CORES)
    other = 1 - c
    q = xy * CORES + c
    zr = rem(z + xy, Z)
    right = rem(z + 1, Z)
    left = rem(z + Z - 1, Z)
    twin = (z * CORES + other, xy)

    def plane_peer(q2):
        return (z * CORES + rem(q2, CORES), div(q2, CORES))

    def target(k):
        i, n = div(k, S * CORES), rem(k, S * CORES)
        distance = HZ + div(i + 1, 2) * (1 - 2 * rem(i, 2))
        owner = rem(div(xy, S) - z - distance + 2 * Z, Z) + div(n, CORES) * Z
        return owner * CORES + rem(c + n, CORES)

    def issue(which, first, last):
        def body(k):
            q2 = target(k)

            @pl.when(q2 != q)
            def _():
                rows_copy(which, q2).start()

        loop(first * S * CORES, last * S * CORES, body)

    def each_source(t, action):
        def body(n):
            q2 = t * (S * CORES) + n
            pl.when(q2 != q)(lambda: action(q2))

        loop(0, S * CORES, body)

    barrier = pltpu.get_barrier_semaphore()

    def greet_plane(k):
        pl.semaphore_signal(
            barrier, inc=1, device_id=plane_peer(rem(q + k, NQ)), device_id_type=MESH
        )

    def greet_column(m):
        z2 = rem(z + 1 + div(m, CORES), Z)
        pl.semaphore_signal(
            barrier, inc=1, device_id=(z2 * CORES + rem(m, CORES), xy), device_id_type=MESH
        )

    loop(1, NQ, greet_plane)
    loop(0, CORES * (Z - 1), greet_column)

    def own_weights(i, src, dst):
        return pltpu.make_async_copy(src, dst, wl_s.at[i])

    half = pl.ds(pl.multiple_of(c * W, W), W)
    mine = pl.ds(c * 2, 2)
    theirs = pl.ds(other * 2, 2)
    own_copies = [
        own_weights(0, w_gate.at[mine], wg.at[:, half, :]),
        own_weights(1, w_up.at[mine], wu.at[:, half, :]),
        own_weights(2, w_down.at[mine], wd.at[c]),
    ]
    for copy in own_copies:
        copy.start()

    route = routing[...]
    row_e = lax.broadcasted_iota(jnp.int32, (E, TOK), 0)
    has = jnp.zeros((E, TOK), F32)
    for k in range(route.shape[0]):
        has = has + jnp.where(route[k : k + 1, :] == row_e, 1.0, 0.0)
    t_row = lax.broadcasted_iota(jnp.int32, (TOK, TOK), 0)
    t_col = lax.broadcasted_iota(jnp.int32, (TOK, TOK), 1)
    before = jnp.where(t_row < t_col, 1.0, 0.0).astype(BF)
    same = jnp.where(t_row == t_col, 1.0, 0.0).astype(BF)
    pos = jnp.where(has > 0.5, dot_nn(has.astype(BF), before), -1.0)
    chosen_ref[...] = dot_nt(same, has.astype(BF))
    slot_iota = lax.broadcasted_iota(jnp.int32, (E, CAP, TOK), 1).astype(F32)
    placing = jnp.where(pos[:, None, :] == slot_iota, 1.0, 0.0)
    placing = placing.reshape(E * CAP, TOK).astype(BF)
    place[...] = placing.reshape(NE, CORES, PAIR, TOK)
    send_rows[0] = dot_nn(placing, tokens[...]).astype(BF).reshape(NQ, PAIR, W)
    send_rows[1] = dot_nn(placing, cotangent[...]).astype(BF).reshape(NQ, PAIR, W)

    pl.semaphore_wait(barrier, NQ - 1 + CORES * (Z - 1))

    def rows_copy(which, q2):
        return remote(
            send_rows.at[which, q2], in_rows.at[which, c, xy],
            rows_s.at[which, q2], rows_r.at[which, q], plane_peer(q2),
        )

    def rows_arrival(which, q2):
        return remote(
            send_rows.at[which, q2], in_rows.at[which, rem(q2, CORES), div(q2, CORES)],
            rows_s.at[which, q2], rows_r.at[which, q2], plane_peer(q2),
        )

    weight_copies = [
        remote(w_gate.at[theirs], wg.at[:, half, :], wx_s.at[0], wx_r.at[0], twin),
        remote(w_up.at[theirs], wu.at[:, half, :], wx_s.at[1], wx_r.at[1], twin),
        remote(w_down.at[theirs], wd.at[c], wx_s.at[2], wx_r.at[2], twin),
    ]
    other_half = pl.ds(pl.multiple_of(other * W, W), W)
    weight_arrivals = [
        remote(w_gate.at[theirs], wg.at[:, other_half, :], wx_s.at[0], wx_r.at[0], twin),
        remote(w_up.at[theirs], wu.at[:, other_half, :], wx_s.at[1], wx_r.at[1], twin),
        remote(w_down.at[theirs], wd.at[other], wx_s.at[2], wx_r.at[2], twin),
    ]
    weight_copies[0].start()
    weight_copies[1].start()
    issue(0, 0, ROWS_FIRST)
    in_rows[0, c, xy] = send_rows[0, q]
    in_rows[1, c, xy] = send_rows[1, q]

    def sum_blocks(n, index, peer, src, into, out, sem_s, sem_r):
        def scatter(j):
            return remote(src.at[j], into.at[index], sem_s.at[0, j], sem_r.at[0, index], peer(j))

        def scatter_arrival(j):
            return remote(src.at[j], into.at[j], sem_s.at[0, j], sem_r.at[0, j], peer(j))

        def gather(j):
            return remote(
                out.at[index], out.at[index], sem_s.at[1, j], sem_r.at[1, index], peer(j)
            )

        def gather_arrival(j):
            return remote(out.at[j], out.at[j], sem_s.at[1, j], sem_r.at[1, j], peer(j))

        def send():
            loop(1, n, lambda k: scatter(rem(index + k, n)).start())
            into[index] = src[index]

        def reduce():
            loop(1, n, lambda k: scatter_arrival(rem(index + k, n)).wait_recv())
            out[index] = jnp.sum(into[...], axis=0)
            loop(1, n, lambda k: gather(rem(index + k, n)).start())

        def finish():
            loop(1, n, lambda k: gather_arrival(rem(index + k, n)).wait_recv())

        def drain():
            loop(1, n, lambda k: scatter(rem(index + k, n)).wait_send())
            loop(1, n, lambda k: gather(rem(index + k, n)).wait_send())

        return send, reduce, finish, drain

    p1_send, p1_reduce, p1_finish, p1_drain = sum_blocks(
        ND, dp, lambda j: (j, xy), sum_src, sum_in, sum_out, p1_s, p1_r
    )
    p2_send, p2_reduce, p2_finish, p2_drain = sum_blocks(
        NE, xy, lambda j: (dp, j), gr_src, gr_in, gr_out, p2_s, p2_r
    )

    p3_send, p3_reduce, p3_finish, p3_drain = sum_blocks(
        ND, dp, lambda j: (j, xy), top_src, top_parts, top_out, p3_s, p3_r
    )

    def packed(first, second, count):
        if E < EL:
            gap = jnp.zeros((TOK, EL - E), F32)
            first = jnp.concatenate([first, gap], axis=1)
            second = jnp.concatenate([second, gap], axis=1)
        return jnp.concatenate([first, second], axis=1).reshape(count, TOK // count, 2 * EL)

    logits_part = dot_nt(tokens[...], w_router[...])
    mean_part = dot_nt(cotangent[...], running_mean[...])
    sum_src[...] = packed(logits_part, mean_part, ND)
    p1_send()

    def order_rows(which, t):
        each_source(t, lambda q2: rows_arrival(which, q2).wait_recv())
        at = pl.ds(pl.multiple_of(t * SC, SC), SC)
        for h in range(CORES):
            block = in_rows[which, h, pl.ds(t * S, S)].astype(F32)
            for j in range(2):
                piece = block[:, j * CAP : (j + 1) * CAP, :].reshape(SC, W)
                rows[which, j, at, h * W : (h + 1) * W] = piece.astype(BF)

    def some_rows(which, j, places):
        return jnp.concatenate(
            [rows[which, j, pl.ds(pl.multiple_of(t * SC, SC), SC), :] for t in places], axis=0
        )

    def forward_parts(*places, ordered=False):
        for t in places:
            if not ordered:
                order_rows(0, t)
        for j in range(2):
            x = some_rows(0, j, places)
            for r in range(2):
                cols = slice(r * HH, (r + 1) * HH)
                gate = dot_nn(x, wg[j, :, cols]).astype(BF)
                up = dot_nn(x, wu[j, :, cols]).astype(BF)
                for i, t in enumerate(places):
                    part[j, t, r, :, 0:HH] = gate[i * SC : (i + 1) * SC]
                    part[j, t, r, :, HH:H] = up[i * SC : (i + 1) * SC]

    def backward_parts(*places):
        for t in places:
            order_rows(1, t)
        for j in range(2):
            x = some_rows(1, j, places)
            for r in range(2):
                units = slice(r * HH, (r + 1) * HH)
                value = dot_nt(x[:, 0:W], wd[0, j, units, :]) + dot_nt(
                    x[:, W : 2 * W], wd[1, j, units, :]
                )
                value = value.astype(BF)
                for i, t in enumerate(places):
                    part[2, t, r, :, j * HH : (j + 1) * HH] = value[i * SC : (i + 1) * SC]

    def ring_peer(r):
        return ((right if r == 0 else left) * CORES + c, xy)

    def rs_copy(k, r, s):
        t = rem(zr + HZ - s, Z) if r == 0 else rem(zr - HZ + s + Z, Z)
        if s == 0:
            src, dst = part.at[k, t, r], recv.at[k, r, 0, r]
        else:
            src, dst = part.at[k, t], recv.at[k, r, s]
        return remote(src, dst, rs_s.at[k, r, s], rs_r.at[k, r, s], ring_peer(r))

    def rs_step(k, s):
        for r in range(2):
            rs_copy(k, r, s).wait_recv()
            t = rem(zr + HZ - s - 1, Z) if r == 0 else rem(zr - HZ + s + 1 + Z, Z)
            if s == 0:
                part[k, t, r] = (part[k, t, r].astype(F32) + recv[k, r, 0, r].astype(F32)).astype(BF)
            else:
                part[k, t] = (part[k, t].astype(F32) + recv[k, r, s].astype(F32)).astype(BF)
            rs_copy(k, r, s + 1).start()

    def rs_start(k):
        for r in range(2):
            rs_copy(k, r, 0).start()

    def rs_end(k):
        for r in range(2):
            rs_copy(k, r, HZ - 1).wait_recv()

    def ag_copy(k, r, s):
        t = rem(zr - s + Z, Z) if r == 0 else rem(zr + s, Z)
        ref = full.at[k, t, r] if s == HZ - 1 else full.at[k, t]
        return remote(ref, ref, ag_s.at[k, r, s], ag_r.at[k, r, s], ring_peer(r))

    def ag_arrival(k, r, s):
        t = rem(zr - 1 - s + Z, Z) if r == 0 else rem(zr + 1 + s, Z)
        ref = full.at[k, t, r] if s == HZ - 1 else full.at[k, t]
        return remote(ref, ref, ag_s.at[k, r, s], ag_r.at[k, r, s], ring_peer(r))

    def ag_step(k, s):
        for r in range(2):
            ag_arrival(k, r, s).wait_recv()
            if s < HZ - 1:
                ag_copy(k, r, s + 1).start()

    def ag_start(k):
        for r in range(2):
            ag_copy(k, r, 0).start()

    def two_places(distance):
        return rem(zr + distance, Z), rem(zr - distance + Z, Z)

    def backward_start():
        own_copies[2].wait()
        weight_arrivals[2].wait_recv()
        backward_parts(rem(zr + HZ, Z))
        rs_start(2)

    own_copies[0].wait()
    own_copies[1].wait()
    weight_arrivals[0].wait_recv()
    weight_arrivals[1].wait_recv()
    order_rows(0, rem(zr + HZ, Z))
    issue(0, ROWS_FIRST, Z)
    weight_copies[2].start()
    issue(1, 0, GRADS_FIRST)
    forward_parts(rem(zr + HZ, Z), ordered=True)
    rs_start(0)
    rs_start(1)
    p1_reduce()
    for s in range(HZ - 1):
        forward_parts(*two_places(HZ - 1 - s))
        for j in range(2):
            rs_step(j, s)
        if s == 0:
            issue(1, GRADS_FIRST, GRADS_NEXT)
        if s == max(HZ - 3, 0):
            issue(1, GRADS_NEXT, Z)
            backward_start()
    forward_parts(zr)
    backward_parts(*two_places(HZ - 1))
    rs_step(2, 0)

    p1_finish()
    sums = sum_out[...].reshape(TOK, 2 * EL)
    weights_exp = jnp.exp(sums[:, 0:E])
    prob_ref[...] = weights_exp / jnp.sum(weights_exp, axis=1, keepdims=True)

    spot = rem(xy, S)
    first_owner = rem(div(xy, S) - z + Z, Z)
    owners = [first_owner + m * Z for m in range(S)]
    pair_row = lax.broadcasted_iota(jnp.int32, (PAIR, 2 * EL), 0)
    pair_lane = lax.broadcasted_iota(jnp.int32, (PAIR, 2 * EL), 1)
    pair_expert = c * 2 + jnp.where(pair_row >= CAP, 1, 0)

    def w_copy(m):
        return remote(
            w_send.at[m], w_in.at[spot], wt_s.at[m], wt_r.at[spot], (dp, owners[m])
        )

    def w_arrival(b):
        return remote(w_send.at[b], w_in.at[b], wt_s.at[b], wt_r.at[b], (dp, zr * S + b))

    for m in range(S):
        spread = dot_nn(place[owners[m], c], prob_ref[...].astype(BF))
        if E < 2 * EL:
            spread = jnp.concatenate([spread, jnp.zeros((PAIR, 2 * EL - E), F32)], axis=1)
        spread = jnp.where(pair_lane == owners[m] * 4 + pair_expert, spread, 0.0)
        column = jnp.sum(spread, axis=1, keepdims=True)
        w_send[m] = jnp.broadcast_to(column, (PAIR, 2 * EL)).astype(BF)

        @pl.when(owners[m] != xy)
        def _(m=m):
            w_copy(m).start()

        @pl.when(owners[m] == xy)
        def _(m=m):
            w_in[spot] = w_send[m]

    for s in range(1, HZ - 1):
        backward_parts(*two_places(HZ - 1 - s))
        rs_step(2, s)
    backward_parts(zr)

    for b in range(S):

        @pl.when(zr * S + b != xy)
        def _(b=b):
            w_arrival(b).wait_recv()

    for k in range(3):
        rs_end(k)

    def total(k, r, cols):
        value = part[k, zr, r, :, cols].astype(F32)
        return (
            value
            + recv[k, 0, HZ - 1, r, :, cols].astype(F32)
            + recv[k, 1, HZ - 1, r, :, cols].astype(F32)
        )

    dots = []
    for j in range(2):
        weight = jnp.concatenate(
            [w_in[b].astype(F32)[j * CAP : (j + 1) * CAP, 0:1] for b in range(S)], axis=0
        )
        dot = jnp.zeros((SC, 1), F32)
        for r in range(2):
            cols = slice(j * HH, (j + 1) * HH)
            raw = total(2, r, cols)
            gate = total(j, r, slice(0, HH))
            up = total(j, r, slice(HH, H))
            sig = 1.0 / (1.0 + jnp.exp(-gate))
            silu = gate * sig
            hidden = silu * up
            d_hidden = raw * weight
            full[j, zr, r, :, 0:HH] = (
                d_hidden * up * sig * (1.0 + gate * (1.0 - sig))
            ).astype(BF)
            full[j, zr, r, :, HH:H] = (d_hidden * silu).astype(BF)
            full[2, zr, r, :, cols] = (hidden * weight).astype(BF)
            dot = dot + jnp.sum(hidden * raw, axis=1, keepdims=True)
        ag_start(j)
        dots.append(dot)
    ag_start(2)

    def dots_copy(b):
        return remote(
            dots_send.at[b], dots_in.at[div(xy, Z)], dt_s.at[b], dt_r.at[div(xy, Z)], (dp, zr * S + b)
        )

    def dots_arrival(m):
        return remote(dots_send.at[m], dots_in.at[m], dt_s.at[m], dt_r.at[m], (dp, owners[m]))

    for b in range(S):
        value = jnp.concatenate(
            [dots[0][b * CAP : (b + 1) * CAP], dots[1][b * CAP : (b + 1) * CAP]], axis=0
        )
        value = jnp.broadcast_to(value, (PAIR, 2 * EL))
        high = value.astype(BF).astype(F32)
        dots_send[b] = jnp.where(pair_lane < EL, high, value - high).astype(BF)

        @pl.when(zr * S + b != xy)
        def _(b=b):
            dots_copy(b).start()

        @pl.when(zr * S + b == xy)
        def _(b=b):
            dots_in[div(xy, Z)] = dots_send[b]

    def back_copy(q2):
        return remote(
            back_send.at[div(q2, CORES), rem(q2, CORES)], back_in.at[q],
            bk_s.at[q2], bk_r.at[q], plane_peer(q2),
        )

    def back_arrival(q2):
        return remote(
            back_send.at[div(q2, CORES), rem(q2, CORES)], back_in.at[q2],
            bk_s.at[q2], bk_r.at[q2], plane_peer(q2),
        )

    def send_back(*places):
        values = []
        for j in range(2):
            value = None
            for r in range(2):
                cols = slice(r * HH, (r + 1) * HH)
                both = jnp.concatenate([full[j, t, r] for t in places], axis=0)
                term = dot_nt(both[:, 0:HH], wg[j, :, cols]) + dot_nt(
                    both[:, HH:H], wu[j, :, cols]
                )
                value = term if value is None else value + term
            values.append(value)
        for i, t in enumerate(places):
            for b in range(S):
                at = slice(i * SC + b * CAP, i * SC + (b + 1) * CAP)
                block = jnp.concatenate([values[0][at], values[1][at]], axis=0).astype(BF)
                for h in range(CORES):
                    source = t * S + b
                    q2 = source * CORES + h
                    back_send[source, h] = block[:, h * W : (h + 1) * W]

                    @pl.when(q2 != q)
                    def _(q2=q2):
                        back_copy(q2).start()

                    @pl.when(q2 == q)
                    def _(source=source, h=h):
                        back_in[q] = back_send[source, h]

    def send_dots():
        for m in range(S):

            @pl.when(owners[m] != xy)
            def _(m=m):
                dots_arrival(m).wait_recv()

        top = None
        for m in range(S):
            lane_e = jnp.where(pair_lane >= EL, pair_lane - EL, pair_lane)
            masked = jnp.where(
                lane_e == owners[m] * 4 + pair_expert, dots_in[m].astype(F32), 0.0
            ).astype(BF)
            term = dot_tn(place[owners[m], c], masked)
            top = term if top is None else top + term
        top_src[...] = top.reshape(ND, TOK // ND, 2 * EL)
        p3_send()

    def router_gradients():
        p3_finish()
        top = top_out[...].reshape(TOK, 2 * EL)
        top = top[:, 0:E] + top[:, EL : EL + E]
        mean = sum_out[...].reshape(TOK, 2 * EL)[:, EL : EL + E]
        d_prob = jnp.where(chosen_ref[...] > 0.5, top, mean)
        prob = prob_ref[...]
        dlogits = prob * (d_prob - jnp.sum(prob * d_prob, axis=1, keepdims=True))
        high, low = split_two(dlogits)
        dlog_hi[...] = high
        dlog_lo[...] = low
        router_part = dot_tn(high, tokens[...]) + dot_tn(low, tokens[...])
        for h in range(W // 128):
            gr_src[h * GB : (h + 1) * GB] = router_part[:, h * 128 : (h + 1) * 128].reshape(
                GB, E // GB, 128
            )
        p2_send()

    actions = [send_dots, p3_reduce, router_gradients, p2_reduce]
    send_back(zr)
    for s in range(HZ):
        for j in range(2):
            ag_step(j, s)
        if s < HZ - 1:
            send_back(*two_places(1 + s))
            ag_step(2, s)
            actions[s]()
        else:
            send_back(rem(zr + HZ, Z))
            for action in actions[s:]:
                action()

    def give(i, j):
        out = (grad_gate, grad_up, grad_down)[i]
        buf = (out_gate, out_up, out_down)[i]
        return remote(
            buf.at[j], out.at[c * 2 + j], ox_s.at[i, j], ox_r.at[i, j], twin
        )

    def take(i, j):
        out = (grad_gate, grad_up, grad_down)[i]
        buf = (out_gate, out_up, out_down)[i]
        return remote(
            buf.at[j], out.at[other * 2 + j], ox_s.at[i, j], ox_r.at[i, j], twin
        )

    for mine_now in (False, True):
        features = half if mine_now else other_half
        for j in range(2):
            x = rows[0, j, :, features]
            for r in range(2):
                cols = slice(r * HH, (r + 1) * HH)
                both = full[j, :, r].reshape(ROWS, H)
                gate = dot_tn(x, both[:, 0:HH]).astype(BF)
                up = dot_tn(x, both[:, HH:H]).astype(BF)
                if mine_now:
                    grad_gate[c * 2 + j, :, cols] = gate
                    grad_up[c * 2 + j, :, cols] = up
                else:
                    out_gate[j, :, cols] = gate
                    out_up[j, :, cols] = up
            if not mine_now:
                give(0, j).start()
                give(1, j).start()
        if not mine_now:
            ag_step(2, HZ - 1)
        for j in range(2):
            x = rows[1, j, :, features]
            for r in range(2):
                units = slice(r * HH, (r + 1) * HH)
                hid = full[2, :, r, :, j * HH : (j + 1) * HH].reshape(ROWS, HH)
                down = dot_tn(hid, x).astype(BF)
                if mine_now:
                    grad_down[c * 2 + j, units, :] = down
                else:
                    out_down[j, units, :] = down
            if not mine_now:
                give(2, j).start()

    loop(1, NQ, lambda k: back_arrival(rem(q + k, NQ)).wait_recv())
    router_term = dot_nn(dlog_hi[...], w_router[...]) + dot_nn(dlog_lo[...], w_router[...])
    token_term = dot_tn(
        place[...].reshape(E * CAP, TOK), back_in[...].reshape(E * CAP, W)
    )
    grad_tokens[...] = (token_term + router_term).astype(BF)
    p2_finish()
    for h in range(W // 128):
        grad_router[:, h * 128 : (h + 1) * 128] = gr_out[h * GB : (h + 1) * GB].reshape(E, 128)

    loop(1, NQ, lambda k: rows_copy(0, rem(q + k, NQ)).wait_send())
    loop(1, NQ, lambda k: rows_copy(1, rem(q + k, NQ)).wait_send())
    loop(1, NQ, lambda k: back_copy(rem(q + k, NQ)).wait_send())
    for copy in weight_copies:
        copy.wait_send()
    p1_drain()
    p2_drain()
    p3_drain()

    for k in range(3):
        for r in range(2):
            for s in range(HZ):
                rs_copy(k, r, s).wait_send()
                ag_copy(k, r, s).wait_send()

    for m in range(S):

        @pl.when(owners[m] != xy)
        def _(m=m):
            w_copy(m).wait_send()

    for b in range(S):

        @pl.when(zr * S + b != xy)
        def _(b=b):
            dots_copy(b).wait_send()

    for i in range(3):
        for j in range(2):
            give(i, j).wait_send()
            take(i, j).wait_recv()


def per_device(tokens, cotangent, routing, w_router, running_mean, w_gate, w_up, w_down):
    NE = lax.axis_size("expert")
    ND = lax.axis_size("dp")
    Z = ND // CORES
    local_count, W, H = w_gate.shape
    E = NE * local_count
    TOK, top = routing.shape
    routing, w_router = routing.T, w_router.T
    CAP = 3 * TOK * top // (2 * E)
    NQ = NE * CORES
    S = NE // Z
    HZ = Z // 2
    PAIR, ROWS = 2 * CAP, NE * CAP
    sizes = (NE, Z, E, TOK, H, W, CAP)
    vmem = pl.BlockSpec(memory_space=pltpu.VMEM)
    hbm = pl.BlockSpec(memory_space=pl.ANY)
    dma = pltpu.SemaphoreType.DMA
    scratch = [
        pltpu.VMEM((NE, CORES, PAIR, TOK), BF),
        pltpu.VMEM((2, NQ, PAIR, W), BF),
        pltpu.VMEM((2, CORES, NE, PAIR, W), BF),
        pltpu.VMEM((2, 2, ROWS, 2 * W), BF),
        pltpu.VMEM((2, 2 * W, H), BF),
        pltpu.VMEM((2, 2 * W, H), BF),
        pltpu.VMEM((2, 2, H, W), BF),
        pltpu.VMEM((3, Z, 2, S * CAP, H), BF),
        pltpu.VMEM((3, 2, HZ, 2, S * CAP, H), BF),
        pltpu.VMEM((3, Z, 2, S * CAP, H), BF),
        pltpu.VMEM((ND, TOK // ND, 128), F32),
        pltpu.VMEM((ND, TOK // ND, 128), F32),
        pltpu.VMEM((ND, TOK // ND, 128), F32),
        pltpu.VMEM((NE, E * W // (128 * NE), 128), F32),
        pltpu.VMEM((NE, E * W // (128 * NE), 128), F32),
        pltpu.VMEM((NE, E * W // (128 * NE), 128), F32),
        pltpu.VMEM((ND, TOK // ND, 128), F32),
        pltpu.VMEM((ND, TOK // ND, 128), F32),
        pltpu.VMEM((ND, TOK // ND, 128), F32),
        pltpu.VMEM((TOK, E), F32),
        pltpu.VMEM((TOK, E), F32),
        pltpu.VMEM((S, PAIR, 128), BF),
        pltpu.VMEM((S, PAIR, 128), BF),
        pltpu.VMEM((S, PAIR, 128), BF),
        pltpu.VMEM((S, PAIR, 128), BF),
        pltpu.VMEM((TOK, E), BF),
        pltpu.VMEM((TOK, E), BF),
        pltpu.VMEM((NE, CORES, PAIR, W), BF),
        pltpu.VMEM((NQ, PAIR, W), BF),
        pltpu.VMEM((2, W, H), BF),
        pltpu.VMEM((2, W, H), BF),
        pltpu.VMEM((2, H, W), BF),
        dma((2, NQ)), dma((2, NQ)),
        dma((3,)), dma((3,)), dma((3,)),
        dma((2, ND)), dma((2, ND)),
        dma((2, NE)), dma((2, NE)),
        dma((2, ND)), dma((2, ND)),
        dma((3, 2, HZ)), dma((3, 2, HZ)),
        dma((3, 2, HZ)), dma((3, 2, HZ)),
        dma((S,)), dma((S,)),
        dma((S,)), dma((S,)),
        dma((NQ,)), dma((NQ,)),
        dma((3, 2)), dma((3, 2)),
    ]
    results = pl.pallas_call(
        functools.partial(kernel, sizes),
        out_shape=(
            pltpu.VMEM((TOK, W), BF),
            pltpu.VMEM((E, W), F32),
            pltpu.VMEM((local_count, W, H), BF),
            pltpu.VMEM((local_count, W, H), BF),
            pltpu.VMEM((local_count, H, W), BF),
        ),
        in_specs=[vmem] * 5 + [hbm] * 3,
        out_specs=(vmem, vmem, vmem, vmem, vmem),
        scratch_shapes=scratch,
        compiler_params=pltpu.CompilerParams(
            collective_id=0, has_side_effects=True, vmem_limit_bytes=56 * 1024 * 1024
        ),
        cost_estimate=pl.CostEstimate(
            flops=6 * 10**9, bytes_accessed=10**7, transcendentals=10**5
        ),
    )(tokens, cotangent, routing, w_router, running_mean, w_gate, w_up, w_down)
    grad_tokens, grad_router, *rest = results
    return (grad_tokens, grad_router.T, *rest)


def solution(mesh):
    return jax.shard_map(
        per_device,
        mesh=mesh,
        in_specs=(
            P("expert", "dp"),
            P("expert", "dp"),
            P("expert", None),
            P("dp", None),
            P(None, "dp"),
            P("expert", "dp", None),
            P("expert", "dp", None),
            P("expert", None, "dp"),
        ),
        out_specs=(
            P("expert", "dp"),
            P("dp", None),
            P("expert", "dp", None),
            P("expert", "dp", None),
            P("expert", None, "dp"),
        ),
        check_vma=False,
    )
```

time: 287 us -> 119 us (0.41)
  Pallas kernels: 281 us -> 113 us
    pallas_call x1 -> x0, Pallas kernels: 148 us -> none  [per_device(): pl.pallas_call(write_out, out_shape=[jax.ShapeDtypeStruct(x.shape, x.dtyp...]
    pallas_call x1, Pallas kernels: 133 us -> 113 us  [per_device(): pl.pallas_call(functools.partial(kernel, sizes), out_shape=(pltpu.VMEM((T...]
where the time goes in v3:
time: 119 us; the launch traced here: 118 us
  Pallas kernels  113 us (95%)
  local copies, waits for them, and re-layouts  4.69 us (4%)
    pallas_call x1, Pallas kernels, per_device(): pl.pallas_call(functools.partial(kernel, sizes), out_shape=(pltpu.VMEM((T...  113 us
    unnamed x5, local copies, waits for them, and re-layouts  4.69 us

profile of v3, /device:TPU:2, one launch (start us, length us, event | category | flops | bytes accessed | tf_op | source)
XLA Modules:
  0.0 118.4 jit_solution(7573618750709598240)
XLA Ops:
  0.6 113.1 %shard_map.119 = (bf16[128,256]{1,0:T(8,128)(2,1)S(1)}, f32[64,256]{1,0:T(8,128)S(1)}, bf16[4,256,768]{2,1,0:T(8,128)(2,1)S(1)}, bf16[4,256,768]{2,1,0:T(8,128)(2,1)S(1)}, bf16[4,768,256]{2,1,0:T(8,128)(2,1)S(1)}) custom-call(bf16[128,256]{1,0:T(8,128)(2,1)} %tokens.1, bf16[128,256]{1,0:T(8,128)(2,1)} %cotangent.1, s32[8,128]{1,0:T(8,128)} %bitcast.5, ...), custom_call_target="tpu_custom_call" | custom-call | flops 6000000000 | bytes 10000000 | tf_op jit(solution)/shard_map/pallas_call | solution.py:739
  113.7 0.6 copy.18
  114.3 0.6 copy.19
  115.0 1.1 copy.20
  116.1 1.1 copy.21
  117.2 1.1 copy.22

commit v4 on v3

--- a/solution.py
+++ b/solution.py
@@ -12,8 +12,10 @@
 F32 = jnp.float32
 CORES = 2
 ROWS_FIRST = 3
-GRADS_FIRST = 0
+ROWS_NEXT = 8
+GRADS_FIRST = 1
 GRADS_NEXT = 4
+BACK_AT = 0
 
 
 def rem(a, n):
@@ -66,13 +68,12 @@
     tokens, cotangent, routing, w_router, running_mean, w_gate, w_up, w_down,
     grad_tokens, grad_router, grad_gate, grad_up, grad_down,
     place, send_rows, in_rows, rows, wg, wu, wd,
-    part, recv, full,
-    sum_src, sum_in, sum_out, gr_src, gr_in, gr_out,
-    top_src, top_parts, top_out,
+    part, recv, full, part_b, recv_b, full_b,
+    sum_src, sum_in, sum_out, gr_src, gx_in, gy_in, gr_out, top_in,
     prob_ref, chosen_ref, w_send, w_in, dots_send, dots_in, dlog_hi, dlog_lo,
     back_send, back_in, out_gate, out_up, out_down,
     rows_s, rows_r, wx_s, wx_r, wl_s,
-    p1_s, p1_r, p2_s, p2_r, p3_s, p3_r,
+    p1_s, p1_r, p2_s, p2_r, tp_s, tp_r,
     rs_s, rs_r, ag_s, ag_r,
     wt_s, wt_r, dt_s, dt_r, bk_s, bk_r,
     ox_s, ox_r,
@@ -85,7 +86,6 @@
     HH = H // 2
     SC = S * CAP
     EL = 64
-    GB = NE // (W // 128)
     PAIR = 2 * CAP
     ROWS = NE * CAP
 
@@ -100,47 +100,54 @@
     left = rem(z + Z - 1, Z)
     twin = (z * CORES + other, xy)
 
-    def plane_peer(q2):
-        return (z * CORES + rem(q2, CORES), div(q2, CORES))
-
-    def target(k):
-        i, n = div(k, S * CORES), rem(k, S * CORES)
+    def in_plane(owner, core):
+        return (z * CORES + core, owner)
+
+    cores = (c, other)
+
+    def each_target(i, action):
         distance = HZ + div(i + 1, 2) * (1 - 2 * rem(i, 2))
-        owner = rem(div(xy, S) - z - distance + 2 * Z, Z) + div(n, CORES) * Z
-        return owner * CORES + rem(c + n, CORES)
+        first = rem(div(xy, S) - z - distance + 2 * Z, Z)
+        for m in range(S):
+            owner = first + m * Z
+            for core in cores:
+                if core is c:
+                    pl.when(owner != xy)(lambda owner=owner, core=core: action(owner, core))
+                else:
+                    action(owner, core)
 
     def issue(which, first, last):
-        def body(k):
-            q2 = target(k)
-
-            @pl.when(q2 != q)
-            def _():
-                rows_copy(which, q2).start()
-
-        loop(first * S * CORES, last * S * CORES, body)
+        loop(
+            first,
+            last,
+            lambda i: each_target(i, lambda o, h: rows_copy(which, o, h).start()),
+        )
 
     def each_source(t, action):
-        def body(n):
-            q2 = t * (S * CORES) + n
-            pl.when(q2 != q)(lambda: action(q2))
-
-        loop(0, S * CORES, body)
+        for b in range(S):
+            source = t * S + b
+            for core in cores:
+                if core is c:
+                    pl.when(source != xy)(lambda source=source, core=core: action(source, core))
+                else:
+                    action(source, core)
 
     barrier = pltpu.get_barrier_semaphore()
 
+    def greet(*device):
+        pl.semaphore_signal(barrier, inc=1, device_id=device, device_id_type=MESH)
+
     def greet_plane(k):
-        pl.semaphore_signal(
-            barrier, inc=1, device_id=plane_peer(rem(q + k, NQ)), device_id_type=MESH
-        )
-
-    def greet_column(m):
-        z2 = rem(z + 1 + div(m, CORES), Z)
-        pl.semaphore_signal(
-            barrier, inc=1, device_id=(z2 * CORES + rem(m, CORES), xy), device_id_type=MESH
-        )
-
-    loop(1, NQ, greet_plane)
-    loop(0, CORES * (Z - 1), greet_column)
+        for core in range(CORES):
+            greet(z * CORES + core, rem(xy + k, NE))
+
+    def greet_column(k):
+        for core in range(CORES):
+            greet(rem(z + k, Z) * CORES + core, xy)
+
+    greet(*twin)
+    loop(1, NE, greet_plane)
+    loop(1, Z, greet_column)
 
     def own_weights(i, src, dst):
         return pltpu.make_async_copy(src, dst, wl_s.at[i])
@@ -176,16 +183,18 @@
 
     pl.semaphore_wait(barrier, NQ - 1 + CORES * (Z - 1))
 
-    def rows_copy(which, q2):
+    def rows_copy(which, owner, core):
+        q2 = owner * CORES + core
         return remote(
             send_rows.at[which, q2], in_rows.at[which, c, xy],
-            rows_s.at[which, q2], rows_r.at[which, q], plane_peer(q2),
-        )
-
-    def rows_arrival(which, q2):
-        return remote(
-            send_rows.at[which, q2], in_rows.at[which, rem(q2, CORES), div(q2, CORES)],
-            rows_s.at[which, q2], rows_r.at[which, q2], plane_peer(q2),
+            rows_s.at[which, q2], rows_r.at[which, q], in_plane(owner, core),
+        )
+
+    def rows_arrival(which, source, core):
+        q2 = source * CORES + core
+        return remote(
+            send_rows.at[which, q2], in_rows.at[which, core, source],
+            rows_s.at[which, q2], rows_r.at[which, q2], in_plane(source, core),
         )
 
     weight_copies = [
@@ -241,13 +250,68 @@
     p1_send, p1_reduce, p1_finish, p1_drain = sum_blocks(
         ND, dp, lambda j: (j, xy), sum_src, sum_in, sum_out, p1_s, p1_r
     )
-    p2_send, p2_reduce, p2_finish, p2_drain = sum_blocks(
-        NE, xy, lambda j: (dp, j), gr_src, gr_in, gr_out, p2_s, p2_r
-    )
-
-    p3_send, p3_reduce, p3_finish, p3_drain = sum_blocks(
-        ND, dp, lambda j: (j, xy), top_src, top_parts, top_out, p3_s, p3_r
-    )
+    side = 4 if NE % 4 == 0 else NE
+    x, y, NY = rem(xy, side), div(xy, side), NE // side
+
+    def gx_copy(j):
+        return remote(
+            gr_src.at[j], gx_in.at[x], p2_s.at[0, j], p2_r.at[0, x], (dp, y * side + j)
+        )
+
+    def gx_arrival(j):
+        return remote(
+            gr_src.at[j], gx_in.at[j], p2_s.at[0, j], p2_r.at[0, j], (dp, y * side + j)
+        )
+
+    def gy_copy(j):
+        return remote(
+            gy_in.at[y], gy_in.at[y], p2_s.at[1, j], p2_r.at[1, y], (dp, j * side + x)
+        )
+
+    def gy_arrival(j):
+        return remote(
+            gy_in.at[j], gy_in.at[j], p2_s.at[1, j], p2_r.at[1, j], (dp, j * side + x)
+        )
+
+    def gz_copy(j):
+        return remote(
+            gr_out.at[x], gr_out.at[x], p2_s.at[2, j], p2_r.at[2, x], (dp, y * side + j)
+        )
+
+    def gz_arrival(j):
+        return remote(
+            gr_out.at[j], gr_out.at[j], p2_s.at[2, j], p2_r.at[2, j], (dp, y * side + j)
+        )
+
+    def p2_send():
+        for k in range(1, side):
+            gx_copy(rem(x + k, side)).start()
+        gx_in[x] = gr_src[x]
+
+    def p2_middle():
+        for k in range(1, side):
+            gx_arrival(rem(x + k, side)).wait_recv()
+        gy_in[y] = jnp.sum(gx_in[...], axis=0)
+        for k in range(1, NY):
+            gy_copy(rem(y + k, NY)).start()
+
+    def p2_reduce():
+        for k in range(1, NY):
+            gy_arrival(rem(y + k, NY)).wait_recv()
+        gr_out[x] = jnp.sum(gy_in[...], axis=0)
+        for k in range(1, side):
+            gz_copy(rem(x + k, side)).start()
+
+    def p2_finish():
+        for k in range(1, side):
+            gz_arrival(rem(x + k, side)).wait_recv()
+
+    def p2_drain():
+        for k in range(1, side):
+            gx_copy(rem(x + k, side)).wait_send()
+            gz_copy(rem(x + k, side)).wait_send()
+        for k in range(1, NY):
+            gy_copy(rem(y + k, NY)).wait_send()
 
     def packed(first, second, count):
         if E < EL:
@@ -262,7 +326,7 @@
     p1_send()
 
     def order_rows(which, t):
-        each_source(t, lambda q2: rows_arrival(which, q2).wait_recv())
+        each_source(t, lambda o, h: rows_arrival(which, o, h).wait_recv())
         at = pl.ds(pl.multiple_of(t * SC, SC), SC)
         for h in range(CORES):
             block = in_rows[which, h, pl.ds(t * S, S)].astype(F32)
@@ -280,11 +344,11 @@
             if not ordered:
                 order_rows(0, t)
         for j in range(2):
-            x = some_rows(0, j, places)
+            some = some_rows(0, j, places)
             for r in range(2):
                 cols = slice(r * HH, (r + 1) * HH)
-                gate = dot_nn(x, wg[j, :, cols]).astype(BF)
-                up = dot_nn(x, wu[j, :, cols]).astype(BF)
+                gate = dot_nn(some, wg[j, :, cols]).astype(BF)
+                up = dot_nn(some, wu[j, :, cols]).astype(BF)
                 for i, t in enumerate(places):
                     part[j, t, r, :, 0:HH] = gate[i * SC : (i + 1) * SC]
                     part[j, t, r, :, HH:H] = up[i * SC : (i + 1) * SC]
@@ -293,35 +357,43 @@
         for t in places:
             order_rows(1, t)
         for j in range(2):
-            x = some_rows(1, j, places)
+            some = some_rows(1, j, places)
             for r in range(2):
                 units = slice(r * HH, (r + 1) * HH)
-                value = dot_nt(x[:, 0:W], wd[0, j, units, :]) + dot_nt(
-                    x[:, W : 2 * W], wd[1, j, units, :]
+                value = dot_nt(some[:, 0:W], wd[0, j, units, :]) + dot_nt(
+                    some[:, W : 2 * W], wd[1, j, units, :]
                 )
                 value = value.astype(BF)
                 for i, t in enumerate(places):
-                    part[2, t, r, :, j * HH : (j + 1) * HH] = value[i * SC : (i + 1) * SC]
+                    part_b[j, t, r] = value[i * SC : (i + 1) * SC]
 
     def ring_peer(r):
         return ((right if r == 0 else left) * CORES + c, xy)
 
+    def sums_of(k):
+        return (part.at[k], recv.at[k]) if k < 2 else (part_b.at[k - 2], recv_b.at[k - 2])
+
+    def gathered(k):
+        return full.at[k] if k < 2 else full_b.at[k - 2]
+
     def rs_copy(k, r, s):
         t = rem(zr + HZ - s, Z) if r == 0 else rem(zr - HZ + s + Z, Z)
+        own, got = sums_of(k)
         if s == 0:
-            src, dst = part.at[k, t, r], recv.at[k, r, 0, r]
+            src, dst = own.at[t, r], got.at[r, 0, r]
         else:
-            src, dst = part.at[k, t], recv.at[k, r, s]
+            src, dst = own.at[t], got.at[r, s]
         return remote(src, dst, rs_s.at[k, r, s], rs_r.at[k, r, s], ring_peer(r))
 
     def rs_step(k, s):
+        own, got = sums_of(k)
         for r in range(2):
             rs_copy(k, r, s).wait_recv()
             t = rem(zr + HZ - s - 1, Z) if r == 0 else rem(zr - HZ + s + 1 + Z, Z)
             if s == 0:
-                part[k, t, r] = (part[k, t, r].astype(F32) + recv[k, r, 0, r].astype(F32)).astype(BF)
+                own[t, r] = (own[t, r].astype(F32) + got[r, 0, r].astype(F32)).astype(BF)
             else:
-                part[k, t] = (part[k, t].astype(F32) + recv[k, r, s].astype(F32)).astype(BF)
+                own[t] = (own[t].astype(F32) + got[r, s].astype(F32)).astype(BF)
             rs_copy(k, r, s + 1).start()
 
     def rs_start(k):
@@ -334,12 +406,12 @@
 
     def ag_copy(k, r, s):
         t = rem(zr - s + Z, Z) if r == 0 else rem(zr + s, Z)
-        ref = full.at[k, t, r] if s == HZ - 1 else full.at[k, t]
+        ref = gathered(k).at[t, r] if s == HZ - 1 else gathered(k).at[t]
         return remote(ref, ref, ag_s.at[k, r, s], ag_r.at[k, r, s], ring_peer(r))
 
     def ag_arrival(k, r, s):
         t = rem(zr - 1 - s + Z, Z) if r == 0 else rem(zr + 1 + s, Z)
-        ref = full.at[k, t, r] if s == HZ - 1 else full.at[k, t]
+        ref = gathered(k).at[t, r] if s == HZ - 1 else gathered(k).at[t]
         return remote(ref, ref, ag_s.at[k, r, s], ag_r.at[k, r, s], ring_peer(r))
 
     def ag_step(k, s):
@@ -360,31 +432,40 @@
         weight_arrivals[2].wait_recv()
         backward_parts(rem(zr + HZ, Z))
         rs_start(2)
+        rs_start(3)
 
     own_copies[0].wait()
     own_copies[1].wait()
     weight_arrivals[0].wait_recv()
     weight_arrivals[1].wait_recv()
     order_rows(0, rem(zr + HZ, Z))
-    issue(0, ROWS_FIRST, Z)
+    issue(0, ROWS_FIRST, ROWS_NEXT)
     weight_copies[2].start()
     issue(1, 0, GRADS_FIRST)
     forward_parts(rem(zr + HZ, Z), ordered=True)
     rs_start(0)
+    forward_parts(*two_places(HZ - 1))
     rs_start(1)
-    p1_reduce()
+    back_at = min(BACK_AT, HZ - 2)
     for s in range(HZ - 1):
-        forward_parts(*two_places(HZ - 1 - s))
-        for j in range(2):
-            rs_step(j, s)
+        if s > 0:
+            forward_parts(*two_places(HZ - 1 - s))
+        rs_step(0, s)
+        if s > back_at:
+            backward_parts(*two_places(HZ - 1 - (s - back_at - 1)))
+            rs_step(2, s - back_at - 1)
+            rs_step(3, s - back_at - 1)
+        rs_step(1, s)
         if s == 0:
+            p1_reduce()
+            issue(0, ROWS_NEXT, Z)
             issue(1, GRADS_FIRST, GRADS_NEXT)
-        if s == max(HZ - 3, 0):
+        if s == min(1, HZ - 2):
             issue(1, GRADS_NEXT, Z)
+        if s == back_at:
             backward_start()
     forward_parts(zr)
-    backward_parts(*two_places(HZ - 1))
-    rs_step(2, 0)
+    back_done = HZ - 2 - back_at
 
     p1_finish()
     sums = sum_out[...].reshape(TOK, 2 * EL)
@@ -422,9 +503,10 @@
         def _(m=m):
             w_in[spot] = w_send[m]
 
-    for s in range(1, HZ - 1):
+    for s in range(back_done, HZ - 1):
         backward_parts(*two_places(HZ - 1 - s))
         rs_step(2, s)
+        rs_step(3, s)
     backward_parts(zr)
 
     for b in range(S):
@@ -433,26 +515,25 @@
         def _(b=b):
             w_arrival(b).wait_recv()
 
-    for k in range(3):
-        rs_end(k)
-
     def total(k, r, cols):
-        value = part[k, zr, r, :, cols].astype(F32)
+        own, got = sums_of(k)
+        value = own[zr, r, :, cols].astype(F32)
         return (
             value
-            + recv[k, 0, HZ - 1, r, :, cols].astype(F32)
-            + recv[k, 1, HZ - 1, r, :, cols].astype(F32)
+            + got[0, HZ - 1, r, :, cols].astype(F32)
+            + got[1, HZ - 1, r, :, cols].astype(F32)
         )
 
     dots = []
     for j in range(2):
+        rs_end(j)
+        rs_end(2 + j)
         weight = jnp.concatenate(
             [w_in[b].astype(F32)[j * CAP : (j + 1) * CAP, 0:1] for b in range(S)], axis=0
         )
         dot = jnp.zeros((SC, 1), F32)
         for r in range(2):
-            cols = slice(j * HH, (j + 1) * HH)
-            raw = total(2, r, cols)
+            raw = total(2 + j, r, slice(0, HH))
             gate = total(j, r, slice(0, HH))
             up = total(j, r, slice(HH, H))
             sig = 1.0 / (1.0 + jnp.exp(-gate))
@@ -463,11 +544,11 @@
                 d_hidden * up * sig * (1.0 + gate * (1.0 - sig))
             ).astype(BF)
             full[j, zr, r, :, HH:H] = (d_hidden * silu).astype(BF)
-            full[2, zr, r, :, cols] = (hidden * weight).astype(BF)
+            full_b[j, zr, r] = (hidden * weight).astype(BF)
             dot = dot + jnp.sum(hidden * raw, axis=1, keepdims=True)
         ag_start(j)
+        ag_start(2 + j)
         dots.append(dot)
-    ag_start(2)
 
     def dots_copy(b):
         return remote(
@@ -493,16 +574,18 @@
         def _(b=b):
             dots_in[div(xy, Z)] = dots_send[b]
 
-    def back_copy(q2):
-        return remote(
-            back_send.at[div(q2, CORES), rem(q2, CORES)], back_in.at[q],
-            bk_s.at[q2], bk_r.at[q], plane_peer(q2),
-        )
-
-    def back_arrival(q2):
-        return remote(
-            back_send.at[div(q2, CORES), rem(q2, CORES)], back_in.at[q2],
-            bk_s.at[q2], bk_r.at[q2], plane_peer(q2),
+    def back_copy(source, core):
+        q2 = source * CORES + core
+        return remote(
+            back_send.at[source, core], back_in.at[q],
+            bk_s.at[q2], bk_r.at[q], in_plane(source, core),
+        )
+
+    def back_arrival(owner, core):
+        q2 = owner * CORES + core
+        return remote(
+            back_send.at[owner, core], back_in.at[q2],
+            bk_s.at[q2], bk_r.at[q2], in_plane(owner, core),
         )
 
     def send_back(*places):
@@ -521,18 +604,31 @@
             for b in range(S):
                 at = slice(i * SC + b * CAP, i * SC + (b + 1) * CAP)
                 block = jnp.concatenate([values[0][at], values[1][at]], axis=0).astype(BF)
+                source = t * S + b
                 for h in range(CORES):
-                    source = t * S + b
-                    q2 = source * CORES + h
                     back_send[source, h] = block[:, h * W : (h + 1) * W]
-
-                    @pl.when(q2 != q)
-                    def _(q2=q2):
-                        back_copy(q2).start()
-
-                    @pl.when(q2 == q)
-                    def _(source=source, h=h):
-                        back_in[q] = back_send[source, h]
+                for core in cores:
+                    if core is other:
+                        back_copy(source, core).start()
+                    else:
+
+                        @pl.when(source != xy)
+                        def _(source=source):
+                            back_copy(source, c).start()
+
+                        @pl.when(source == xy)
+                        def _(source=source):
+                            back_in[q] = back_send[source, c]
+
+    def top_copy(j):
+        return remote(
+            top_in.at[first_owner, c], top_in.at[first_owner, c], tp_s.at[j], tp_r.at[dp], (j, xy)
+        )
+
+    def top_arrival(j):
+        w = rem(div(xy, S) - div(j, CORES) + Z, Z)
+        ref = top_in.at[w, rem(j, CORES)]
+        return remote(ref, ref, tp_s.at[j], tp_r.at[j], (j, xy))
 
     def send_dots():
         for m in range(S):
@@ -543,19 +639,24 @@
 
         top = None
         for m in range(S):
-            lane_e = jnp.where(pair_lane >= EL, pair_lane - EL, pair_lane)
-            masked = jnp.where(
-                lane_e == owners[m] * 4 + pair_expert, dots_in[m].astype(F32), 0.0
-            ).astype(BF)
-            term = dot_tn(place[owners[m], c], masked)
+            row = 2 * m + jnp.where(pair_row >= CAP, 1, 0)
+            lanes = jnp.where(pair_lane >= EL, pair_lane - EL + 4, pair_lane)
+            keep = (lanes == jnp.where(pair_lane >= EL, row + 4, row))
+            masked = jnp.where(keep, dots_in[m].astype(F32), 0.0).astype(BF)
+            term = dot_tn(masked, place[owners[m], c])
             top = term if top is None else top + term
-        top_src[...] = top.reshape(ND, TOK // ND, 2 * EL)
-        p3_send()
+        top_in[first_owner, c] = jnp.concatenate([top[0:4], top[EL : EL + 4]], axis=0)
+        loop(1, ND, lambda k: top_copy(rem(dp + k, ND)).start())
 
     def router_gradients():
-        p3_finish()
-        top = top_out[...].reshape(TOK, 2 * EL)
-        top = top[:, 0:E] + top[:, EL : EL + E]
+        loop(1, ND, lambda k: top_arrival(rem(dp + k, ND)).wait_recv())
+        count = Z * CORES * 8
+        at = lax.broadcasted_iota(jnp.int32, (count, E), 0)
+        expert = lax.broadcasted_iota(jnp.int32, (count, E), 1)
+        group, core, sub = div(at, 8 * CORES), rem(div(at, 8), CORES), rem(at, 4)
+        named = (group + div(sub, 2) * Z) * 4 + core * 2 + rem(sub, 2)
+        pick = jnp.where((named == expert), 1.0, 0.0).astype(BF)
+        top = dot_tn(top_in[...].reshape(count, TOK).astype(BF), pick)
         mean = sum_out[...].reshape(TOK, 2 * EL)[:, EL : EL + E]
         d_prob = jnp.where(chosen_ref[...] > 0.5, top, mean)
         prob = prob_ref[...]
@@ -564,25 +665,22 @@
         dlog_hi[...] = high
         dlog_lo[...] = low
         router_part = dot_tn(high, tokens[...]) + dot_tn(low, tokens[...])
-        for h in range(W // 128):
-            gr_src[h * GB : (h + 1) * GB] = router_part[:, h * 128 : (h + 1) * 128].reshape(
-                GB, E // GB, 128
-            )
+        blocks = jnp.concatenate(
+            [router_part[:, h * 128 : (h + 1) * 128] for h in range(W // 128)], axis=0
+        )
+        gr_src[...] = blocks.reshape(side, E * W // (128 * side), 128)
         p2_send()
 
-    actions = [send_dots, p3_reduce, router_gradients, p2_reduce]
+    actions = [send_dots, router_gradients, p2_middle, p2_reduce]
     send_back(zr)
     for s in range(HZ):
-        for j in range(2):
-            ag_step(j, s)
-        if s < HZ - 1:
-            send_back(*two_places(1 + s))
-            ag_step(2, s)
-            actions[s]()
-        else:
-            send_back(rem(zr + HZ, Z))
-            for action in actions[s:]:
-                action()
+        ag_step(0, s)
+        ag_step(2, s)
+        ag_step(1, s)
+        send_back(*(two_places(1 + s) if s < HZ - 1 else (rem(zr + HZ, Z),)))
+        ag_step(3, s)
+        for action in actions[s : s + 1] if s < HZ - 1 else actions[s:]:
+            action()
 
     def give(i, j):
         out = (grad_gate, grad_up, grad_down)[i]
@@ -601,12 +699,12 @@
     for mine_now in (False, True):
         features = half if mine_now else other_half
         for j in range(2):
-            x = rows[0, j, :, features]
+            some = rows[0, j, :, features]
             for r in range(2):
                 cols = slice(r * HH, (r + 1) * HH)
                 both = full[j, :, r].reshape(ROWS, H)
-                gate = dot_tn(x, both[:, 0:HH]).astype(BF)
-                up = dot_tn(x, both[:, HH:H]).astype(BF)
+                gate = dot_tn(some, both[:, 0:HH]).astype(BF)
+                up = dot_tn(some, both[:, HH:H]).astype(BF)
                 if mine_now:
                     grad_gate[c * 2 + j, :, cols] = gate
                     grad_up[c * 2 + j, :, cols] = up
@@ -616,14 +714,12 @@
             if not mine_now:
                 give(0, j).start()
                 give(1, j).start()
-        if not mine_now:
-            ag_step(2, HZ - 1)
         for j in range(2):
-            x = rows[1, j, :, features]
+            some = rows[1, j, :, features]
             for r in range(2):
                 units = slice(r * HH, (r + 1) * HH)
-                hid = full[2, :, r, :, j * HH : (j + 1) * HH].reshape(ROWS, HH)
-                down = dot_tn(hid, x).astype(BF)
+                hid = full_b[j, :, r].reshape(ROWS, HH)
+                down = dot_tn(hid, some).astype(BF)
                 if mine_now:
                     grad_down[c * 2 + j, units, :] = down
                 else:
@@ -631,26 +727,40 @@
             if not mine_now:
                 give(2, j).start()
 
-    loop(1, NQ, lambda k: back_arrival(rem(q + k, NQ)).wait_recv())
+    def other_devices(action):
+        action(xy, other)
+
+        def body(k):
+            owner = rem(xy + k, NE)
+            for core in range(CORES):
+                action(owner, core)
+
+        loop(1, NE, body)
+
+    other_devices(lambda o, h: back_arrival(o, h).wait_recv())
     router_term = dot_nn(dlog_hi[...], w_router[...]) + dot_nn(dlog_lo[...], w_router[...])
     token_term = dot_tn(
         place[...].reshape(E * CAP, TOK), back_in[...].reshape(E * CAP, W)
     )
     grad_tokens[...] = (token_term + router_term).astype(BF)
     p2_finish()
+    blocks = gr_out[...].reshape(W // 128, E, 128)
     for h in range(W // 128):
-        grad_router[:, h * 128 : (h + 1) * 128] = gr_out[h * GB : (h + 1) * GB].reshape(E, 128)
-
-    loop(1, NQ, lambda k: rows_copy(0, rem(q + k, NQ)).wait_send())
-    loop(1, NQ, lambda k: rows_copy(1, rem(q + k, NQ)).wait_send())
-    loop(1, NQ, lambda k: back_copy(rem(q + k, NQ)).wait_send())
+        grad_router[:, h * 128 : (h + 1) * 128] = blocks[h]
+
+    def sent(owner, core):
+        rows_copy(0, owner, core).wait_send()
+        rows_copy(1, owner, core).wait_send()
+        back_copy(owner, core).wait_send()
+
+    other_devices(sent)
     for copy in weight_copies:
         copy.wait_send()
     p1_drain()
     p2_drain()
-    p3_drain()
-
-    for k in range(3):
+    loop(1, ND, lambda k: top_copy(rem(dp + k, ND)).wait_send())
+
+    for k in range(4):
         for r in range(2):
             for s in range(HZ):
                 rs_copy(k, r, s).wait_send()
@@ -687,6 +797,8 @@
     S = NE // Z
     HZ = Z // 2
     PAIR, ROWS = 2 * CAP, NE * CAP
+    side = 4 if NE % 4 == 0 else NE
+    GR = E * W // (128 * side)
     sizes = (NE, Z, E, TOK, H, W, CAP)
     vmem = pl.BlockSpec(memory_space=pltpu.VMEM)
     hbm = pl.BlockSpec(memory_space=pl.ANY)
@@ -699,18 +811,20 @@
         pltpu.VMEM((2, 2 * W, H), BF),
         pltpu.VMEM((2, 2 * W, H), BF),
         pltpu.VMEM((2, 2, H, W), BF),
-        pltpu.VMEM((3, Z, 2, S * CAP, H), BF),
-        pltpu.VMEM((3, 2, HZ, 2, S * CAP, H), BF),
-        pltpu.VMEM((3, Z, 2, S * CAP, H), BF),
+        pltpu.VMEM((2, Z, 2, S * CAP, H), BF),
+        pltpu.VMEM((2, 2, HZ, 2, S * CAP, H), BF),
+        pltpu.VMEM((2, Z, 2, S * CAP, H), BF),
+        pltpu.VMEM((2, Z, 2, S * CAP, H // 2), BF),
+        pltpu.VMEM((2, 2, HZ, 2, S * CAP, H // 2), BF),
+        pltpu.VMEM((2, Z, 2, S * CAP, H // 2), BF),
         pltpu.VMEM((ND, TOK // ND, 128), F32),
         pltpu.VMEM((ND, TOK // ND, 128), F32),
         pltpu.VMEM((ND, TOK // ND, 128), F32),
-        pltpu.VMEM((NE, E * W // (128 * NE), 128), F32),
-        pltpu.VMEM((NE, E * W // (128 * NE), 128), F32),
-        pltpu.VMEM((NE, E * W // (128 * NE), 128), F32),
-        pltpu.VMEM((ND, TOK // ND, 128), F32),
-        pltpu.VMEM((ND, TOK // ND, 128), F32),
-        pltpu.VMEM((ND, TOK // ND, 128), F32),
+        pltpu.VMEM((side, GR, 128), F32),
+        pltpu.VMEM((side, GR, 128), F32),
+        pltpu.VMEM((NE // side, GR, 128), F32),
+        pltpu.VMEM((side, GR, 128), F32),
+        pltpu.VMEM((Z, CORES, 8, TOK), F32),
         pltpu.VMEM((TOK, E), F32),
         pltpu.VMEM((TOK, E), F32),
         pltpu.VMEM((S, PAIR, 128), BF),
@@ -727,10 +841,10 @@
         dma((2, NQ)), dma((2, NQ)),
         dma((3,)), dma((3,)), dma((3,)),
         dma((2, ND)), dma((2, ND)),
-        dma((2, NE)), dma((2, NE)),
-        dma((2, ND)), dma((2, ND)),
-        dma((3, 2, HZ)), dma((3, 2, HZ)),
-        dma((3, 2, HZ)), dma((3, 2, HZ)),
+        dma((3, NE)), dma((3, NE)),
+        dma((ND,)), dma((ND,)),
+        dma((4, 2, HZ)), dma((4, 2, HZ)),
+        dma((4, 2, HZ)), dma((4, 2, HZ)),
         dma((S,)), dma((S,)),
         dma((S,)), dma((S,)),
         dma((NQ,)), dma((NQ,)),

time: 119 us -> 111 us (0.933)
  Pallas kernels: 113 us -> 104 us
    pallas_call x1, Pallas kernels: 113 us -> 104 us  [per_device(): pl.pallas_call(functools.partial(kernel, sizes), out_shape=(pltpu.VMEM((T...]
where the time goes in v4:
time: 111 us; the launch traced here: 109 us
  Pallas kernels  104 us (94%)
  local copies, waits for them, and re-layouts  4.69 us (4%)
    pallas_call x1, Pallas kernels, per_device(): pl.pallas_call(functools.partial(kernel, sizes), out_shape=(pltpu.VMEM((T...  104 us
    unnamed x5, local copies, waits for them, and re-layouts  4.69 us

profile of v4, /device:TPU:2, one launch (start us, length us, event | category | flops | bytes accessed | tf_op | source)
XLA Modules:
  0.0 109.3 jit_solution(6411390918318744719)
XLA Ops:
  0.6 104.0 %shard_map.119 = (bf16[128,256]{1,0:T(8,128)(2,1)S(1)}, f32[64,256]{1,0:T(8,128)S(1)}, bf16[4,256,768]{2,1,0:T(8,128)(2,1)S(1)}, bf16[4,256,768]{2,1,0:T(8,128)(2,1)S(1)}, bf16[4,768,256]{2,1,0:T(8,128)(2,1)S(1)}) custom-call(bf16[128,256]{1,0:T(8,128)(2,1)} %tokens.1, bf16[128,256]{1,0:T(8,128)(2,1)} %cotangent.1, s32[8,128]{1,0:T(8,128)} %bitcast.5, ...), custom_call_target="tpu_custom_call" | custom-call | flops 6000000000 | bytes 10000000 | tf_op jit(solution)/shard_map/pallas_call | solution.py:853
  104.6 0.6 copy.18
  105.3 0.6 copy.19
  105.9 1.1 %copy.20 = bf16[4,256,768]{2,1,0:T(8,128)(2,1)} copy(bf16[4,256,768]{2,1,0:T(8,128)(2,1)S(1)} %get-tuple-element.17) | data formatting | bytes 3145728
  107.0 1.1 %copy.21 = bf16[4,256,768]{2,1,0:T(8,128)(2,1)} copy(bf16[4,256,768]{2,1,0:T(8,128)(2,1)S(1)} %get-tuple-element.18) | data formatting | bytes 3145728
  108.2 1.1 %copy.22 = bf16[4,768,256]{2,1,0:T(8,128)(2,1)} copy(bf16[4,768,256]{2,1,0:T(8,128)(2,1)S(1)} %get-tuple-element.19) | data formatting | bytes 3145728

commit v5 on v4

--- a/solution.py
+++ b/solution.py
@@ -675,9 +675,9 @@
     send_back(zr)
     for s in range(HZ):
         ag_step(0, s)
-        ag_step(2, s)
         ag_step(1, s)
         send_back(*(two_places(1 + s) if s < HZ - 1 else (rem(zr + HZ, Z),)))
+        ag_step(2, s)
         ag_step(3, s)
         for action in actions[s : s + 1] if s < HZ - 1 else actions[s:]:
             action()

time: 111 us -> 110 us (level)
  no operation moved by 1% of the time
where the time goes in v5:
time: 110 us; the launch traced here: 109 us
  Pallas kernels  104 us (95%)
  local copies, waits for them, and re-layouts  4.69 us (4%)
    pallas_call x1, Pallas kernels, per_device(): pl.pallas_call(functools.partial(kernel, sizes), out_shape=(pltpu.VMEM((T...  104 us
    unnamed x5, local copies, waits for them, and re-layouts  4.69 us

profile of v5, /device:TPU:2, one launch (start us, length us, event | category | flops | bytes accessed | tf_op | source)
XLA Modules:
  0.0 108.9 jit_solution(5605197383841845028)
XLA Ops:
  0.6 103.6 %shard_map.119 = (bf16[128,256]{1,0:T(8,128)(2,1)S(1)}, f32[64,256]{1,0:T(8,128)S(1)}, bf16[4,256,768]{2,1,0:T(8,128)(2,1)S(1)}, bf16[4,256,768]{2,1,0:T(8,128)(2,1)S(1)}, bf16[4,768,256]{2,1,0:T(8,128)(2,1)S(1)}) custom-call(bf16[128,256]{1,0:T(8,128)(2,1)} %tokens.1, bf16[128,256]{1,0:T(8,128)(2,1)} %cotangent.1, s32[8,128]{1,0:T(8,128)} %bitcast.5, ...), custom_call_target="tpu_custom_call" | custom-call | flops 6000000000 | bytes 10000000 | tf_op jit(solution)/shard_map/pallas_call | solution.py:853
  104.2 0.6 copy.18
  104.9 0.6 copy.19
  105.5 1.1 %copy.20 = bf16[4,256,768]{2,1,0:T(8,128)(2,1)} copy(bf16[4,256,768]{2,1,0:T(8,128)(2,1)S(1)} %get-tuple-element.17) | data formatting | bytes 3145728
  106.6 1.1 %copy.21 = bf16[4,256,768]{2,1,0:T(8,128)(2,1)} copy(bf16[4,256,768]{2,1,0:T(8,128)(2,1)S(1)} %get-tuple-element.18) | data formatting | bytes 3145728
  107.8 1.1 %copy.22 = bf16[4,768,256]{2,1,0:T(8,128)(2,1)} copy(bf16[4,768,256]{2,1,0:T(8,128)(2,1)S(1)} %get-tuple-element.19) | data formatting | bytes 3145728
